TPU v7x, 32 devices: a whole 2x2x4 slice. The times are simulated.
32 devices in a mesh: dp: 16 (over z, y, core), tensor: 2 (over x).
Axes of the slice: x: 2, y: 2, z: 4, core: 2. Of those that a mesh axis runs over, the one named last changes fastest.
Arguments:
- inputs: bfloat16 [2, 16, 1024, 768], P(None, 'dp', 'tensor'), may hold values from -6 to 6
- cotangent: bfloat16 [2, 16, 1024, 768], P(None, 'dp', 'tensor'), may hold values from -6 to 6
- lengths: int32 [2, 16], P(None, 'dp'), may hold values from 64 to 1024, as said below
- gain_one: float32 [768], replicated, may hold values from 0.25 to 1.75
- shift_one: float32 [768], replicated, may hold values from -1.75 to 1.75
- qkv_weight: bfloat16 [768, 3, 768], P(None, None, 'tensor'), may hold values from -0.3125 to 0.3125
- qv_bias: float32 [2, 768], P(None, 'tensor'), may hold values from -1.75 to 1.75
- proj_weight: bfloat16 [768, 768], P('tensor'), may hold values from -6 to 6
- proj_bias: float32 [768], replicated, may hold values from -8 to 8
- gain_two: float32 [768], replicated, may hold values from 0.25 to 1.75
- shift_two: float32 [768], replicated, may hold values from -1.75 to 1.75
- fc_weight: bfloat16 [768, 3072], P(None, 'tensor'), may hold values from -0.21875 to 0.21875
- fc_bias: float32 [3072], P('tensor'), may hold values from -1.75 to 1.75
- out_weight: bfloat16 [3072, 768], P('tensor'), may hold values from -0.75 to 0.75
- out_bias: float32 [768], replicated, may hold values from -8 to 8
Outputs:
- outputs: float32 [2, 16, 1024, 768], P(None, 'dp', 'tensor')
- grad_inputs: float32 [2, 16, 1024, 768], P(None, 'dp', 'tensor')
- grad_gain_one: float32 [768], replicated
- grad_shift_one: float32 [768], replicated
- grad_qkv_weight: float32 [768, 3, 768], P(None, None, 'tensor')
- grad_qv_bias: float32 [2, 768], P(None, 'tensor')
- grad_proj_weight: float32 [768, 768], P('tensor')
- grad_proj_bias: float32 [768], replicated
- grad_gain_two: float32 [768], replicated
- grad_shift_two: float32 [768], replicated
- grad_fc_weight: float32 [768, 3072], P(None, 'tensor')
- grad_fc_bias: float32 [3072], P('tensor')
- grad_out_weight: float32 [3072, 768], P('tensor')
- grad_out_bias: float32 [768], replicated
Inputs may be any that keep to these rules, and one draw needn't show every extreme that they name: `lengths`: in every micro-batch one sequence has length exactly 1024; short sequences are rare.
All inputs are finite; a program needn't handle non-finite values.
Results may differ from a plain program's by a relative error of at most 0.014.
Values may be sent and summed in bfloat16 or wider, within the bound.
A program may use at most 256 MiB of HBM per device.

v0:
```python
import jax
import jax.numpy as jnp
from jax import lax
from jax.sharding import PartitionSpec as P

HEADS = 12
HEAD_DIM = 64


norm_eps = 1e-05
branch_scale = 48 ** (-0.5)
masked_value = -1e30
root_coeff = 0.7978845608028654
cubic_coeff = 0.044715


def normalize(rows):
    centered = rows - jnp.mean(rows, axis=-1, keepdims=True)
    inverse = lax.rsqrt(jnp.mean(centered * centered, axis=-1, keepdims=True) + norm_eps)
    return (centered * inverse, inverse)


def norm_backward(grad_normed, normed, inverse, gain):
    scaled_grad = grad_normed * gain
    mean_one = jnp.mean(scaled_grad, axis=-1, keepdims=True)
    mean_two = jnp.mean(scaled_grad * normed, axis=-1, keepdims=True)
    return inverse * (scaled_grad - mean_one - normed * mean_two)


def gelu_pair(values):
    tangent = jnp.tanh(root_coeff * (values + cubic_coeff * values * values * values))
    result = 0.5 * values * (1.0 + tangent)
    slope = 0.5 * (1.0 + tangent) + 0.5 * values * (1.0 - tangent * tangent) * root_coeff * (
        1.0 + 3.0 * cubic_coeff * values * values
    )
    return (result, slope)


def body(
    inputs,
    cotangent,
    lengths,
    gain_one,
    shift_one,
    qkv_weight,
    qv_bias,
    proj_weight,
    proj_bias,
    gain_two,
    shift_two,
    fc_weight,
    fc_bias,
    out_weight,
    out_bias,
):
    model_width = inputs.shape[-1]
    tensor_parts = lax.axis_size("tensor")
    local_rows = inputs.shape[2]
    seq_len = local_rows * tensor_parts
    local_heads = HEADS // tensor_parts
    local_width = local_heads * HEAD_DIM
    block_rows = min(512, seq_len)
    score_scale = HEAD_DIM ** (-0.5)
    row_ids = lax.axis_index("tensor") * local_rows + jnp.arange(local_rows, dtype=jnp.int32)
    key_ids = jnp.arange(seq_len, dtype=jnp.int32)
    qkv_flat = qkv_weight.reshape(model_width, 3 * local_width)
    bias_flat = jnp.concatenate([qv_bias[0], jnp.zeros((local_width,), jnp.float32), qv_bias[1]])
    hidden_width = fc_weight.shape[1]
    grad_gain_one = jnp.zeros((model_width,), jnp.float32)
    grad_shift_one = jnp.zeros((model_width,), jnp.float32)
    grad_proj_bias = jnp.zeros((model_width,), jnp.float32)
    grad_gain_two = jnp.zeros((model_width,), jnp.float32)
    grad_shift_two = jnp.zeros((model_width,), jnp.float32)
    grad_out_bias = jnp.zeros((model_width,), jnp.float32)
    grad_qkv = jnp.zeros((model_width, 3 * local_width), jnp.float32)
    grad_qv = jnp.zeros((2, local_width), jnp.float32)
    grad_proj = jnp.zeros((local_width, model_width), jnp.float32)
    grad_fc = jnp.zeros((model_width, hidden_width), jnp.float32)
    grad_fc_bias = jnp.zeros((hidden_width,), jnp.float32)
    grad_out = jnp.zeros((hidden_width, model_width), jnp.float32)
    output_list = []
    grad_list = []
    batch_count = inputs.shape[0]
    for batch_index in range(batch_count):
        seq_lens = lengths[batch_index]
        seq_count = seq_lens.shape[0]
        rows_in = inputs[batch_index].astype(jnp.float32)
        normed_one, inverse_one = normalize(rows_in)
        local_one = (normed_one * gain_one + shift_one).astype(jnp.bfloat16)
        full_one = lax.all_gather(local_one, "tensor", axis=1, tiled=True)
        projected = (
            jnp.einsum("srd,dk->srk", full_one, qkv_flat, preferred_element_type=jnp.float32)
            + bias_flat
        )
        projected = projected.astype(jnp.bfloat16).reshape(
            seq_count, seq_len, 3, local_heads, HEAD_DIM
        )
        query_all = projected[:, :, 0]
        key_all = projected[:, :, 1]
        value_all = projected[:, :, 2]

        def allowed_for(first_row):
            query_ids = first_row + jnp.arange(block_rows, dtype=jnp.int32)
            causal = key_ids[None, None, :] <= query_ids[None, :, None]
            inside = key_ids[None, None, :] < seq_lens[:, None, None]
            return (causal & inside)[:, None]

        def block_scores(query_block, first_row):
            scores = (
                jnp.einsum(
                    "sqhe,skhe->shqk", query_block, key_all, preferred_element_type=jnp.float32
                )
                * score_scale
            )
            return jnp.where(allowed_for(first_row), scores, masked_value)

        attended_blocks = []
        logsum_blocks = []
        for first_row in range(0, seq_len, block_rows):
            query_block = query_all[:, first_row : first_row + block_rows]
            scores = block_scores(query_block, first_row)
            row_max = jnp.max(scores, axis=-1, keepdims=True)
            expd = jnp.exp(scores - row_max)
            row_total = jnp.sum(expd, axis=-1, keepdims=True)
            weights = (expd / row_total).astype(jnp.bfloat16)
            logsum_blocks.append(row_max + jnp.log(row_total))
            attended_blocks.append(
                jnp.einsum(
                    "shqk,skhe->sqhe", weights, value_all, preferred_element_type=jnp.float32
                )
            )
        attended = (
            jnp.concatenate(attended_blocks, axis=1)
            .astype(jnp.bfloat16)
            .reshape(seq_count, seq_len, local_width)
        )
        attn_part = jnp.einsum(
            "sre,ed->srd", attended, proj_weight, preferred_element_type=jnp.float32
        )
        attn_local = lax.psum_scatter(attn_part, "tensor", scatter_dimension=1, tiled=True)
        resid = rows_in + branch_scale * (attn_local + proj_bias)
        normed_two, inverse_two = normalize(resid)
        local_two = (normed_two * gain_two + shift_two).astype(jnp.bfloat16)
        full_two = lax.all_gather(local_two, "tensor", axis=1, tiled=True)
        hidden_pre = (
            jnp.einsum("srd,df->srf", full_two, fc_weight, preferred_element_type=jnp.float32)
            + fc_bias
        )
        hidden_value, hidden_slope = gelu_pair(hidden_pre)
        hidden_low = hidden_value.astype(jnp.bfloat16)
        mlp_part = jnp.einsum(
            "srf,fd->srd", hidden_low, out_weight, preferred_element_type=jnp.float32
        )
        mlp_local = lax.psum_scatter(
            mlp_part.astype(jnp.bfloat16), "tensor", scatter_dimension=1, tiled=True
        ).astype(jnp.float32)
        output_list.append(resid + branch_scale * (mlp_local + out_bias))
        valid_rows = (row_ids[None, :] < seq_lens[:, None]).astype(jnp.float32)
        grad_out_rows = cotangent[batch_index].astype(jnp.float32) * valid_rows[:, :, None]
        scaled_out = branch_scale * grad_out_rows
        grad_out_bias = grad_out_bias + jnp.sum(scaled_out, axis=(0, 1))
        mlp_grad_local = scaled_out.astype(jnp.bfloat16)
        mlp_grad_full = lax.all_gather(mlp_grad_local, "tensor", axis=1, tiled=True)
        grad_out = grad_out + jnp.einsum(
            "srf,srd->fd", hidden_low, mlp_grad_full, preferred_element_type=jnp.float32
        )
        grad_hidden = jnp.einsum(
            "srd,fd->srf", mlp_grad_full, out_weight, preferred_element_type=jnp.float32
        )
        grad_pre = (grad_hidden * hidden_slope).astype(jnp.bfloat16)
        grad_fc_bias = grad_fc_bias + jnp.sum(grad_pre.astype(jnp.float32), axis=(0, 1))
        grad_fc = grad_fc + jnp.einsum(
            "srd,srf->df", full_two, grad_pre, preferred_element_type=jnp.float32
        )
        norm_two_part = jnp.einsum(
            "srf,df->srd", grad_pre, fc_weight, preferred_element_type=jnp.float32
        )
        norm_two_grad = lax.psum_scatter(norm_two_part, "tensor", scatter_dimension=1, tiled=True)
        grad_gain_two = grad_gain_two + jnp.sum(norm_two_grad * normed_two, axis=(0, 1))
        grad_shift_two = grad_shift_two + jnp.sum(norm_two_grad, axis=(0, 1))
        grad_resid = grad_out_rows + norm_backward(norm_two_grad, normed_two, inverse_two, gain_two)
        scaled_resid = branch_scale * grad_resid
        grad_proj_bias = grad_proj_bias + jnp.sum(scaled_resid, axis=(0, 1))
        attn_grad_local = scaled_resid.astype(jnp.bfloat16)
        attn_grad_full = lax.all_gather(attn_grad_local, "tensor", axis=1, tiled=True)
        grad_proj = grad_proj + jnp.einsum(
            "sre,srd->ed", attended, attn_grad_full, preferred_element_type=jnp.float32
        )
        grad_attended = jnp.einsum(
            "srd,ed->sre", attn_grad_full, proj_weight, preferred_element_type=jnp.float32
        )
        grad_attended = grad_attended.astype(jnp.bfloat16).reshape(
            seq_count, seq_len, local_heads, HEAD_DIM
        )
        grad_keys = jnp.zeros((seq_count, seq_len, local_heads, HEAD_DIM), jnp.float32)
        grad_values = jnp.zeros((seq_count, seq_len, local_heads, HEAD_DIM), jnp.float32)
        grad_query_blocks = []
        for block_index, first_row in enumerate(range(0, seq_len, block_rows)):
            query_block = query_all[:, first_row : first_row + block_rows]
            grad_block = grad_attended[:, first_row : first_row + block_rows]
            scores = block_scores(query_block, first_row)
            weights = jnp.exp(scores - logsum_blocks[block_index])
            grad_weights = jnp.einsum(
                "sqhe,skhe->shqk", grad_block, value_all, preferred_element_type=jnp.float32
            )
            row_dot = jnp.sum(weights * grad_weights, axis=-1, keepdims=True)
            grad_scores = (weights * (grad_weights - row_dot)).astype(jnp.bfloat16)
            grad_values = grad_values + jnp.einsum(
                "shqk,sqhe->skhe",
                weights.astype(jnp.bfloat16),
                grad_block,
                preferred_element_type=jnp.float32,
            )
            grad_keys = grad_keys + jnp.einsum(
                "shqk,sqhe->skhe", grad_scores, query_block, preferred_element_type=jnp.float32
            )
            grad_query_blocks.append(
                jnp.einsum(
                    "shqk,skhe->sqhe", grad_scores, key_all, preferred_element_type=jnp.float32
                )
                * score_scale
            )
        grad_queries = jnp.concatenate(grad_query_blocks, axis=1)
        grad_projected = jnp.stack([grad_queries, grad_keys * score_scale, grad_values], axis=2)
        grad_projected = grad_projected.astype(jnp.bfloat16).reshape(
            seq_count, seq_len, 3 * local_width
        )
        column_sums = jnp.sum(grad_projected.astype(jnp.float32), axis=(0, 1)).reshape(
            3, local_width
        )
        grad_qv = grad_qv + jnp.stack([column_sums[0], column_sums[2]], axis=0)
        grad_qkv = grad_qkv + jnp.einsum(
            "srd,srk->dk", full_one, grad_projected, preferred_element_type=jnp.float32
        )
        norm_one_part = jnp.einsum(
            "srk,dk->srd", grad_projected, qkv_flat, preferred_element_type=jnp.float32
        )
        norm_one_grad = lax.psum_scatter(
            norm_one_part.astype(jnp.bfloat16), "tensor", scatter_dimension=1, tiled=True
        ).astype(jnp.float32)
        grad_gain_one = grad_gain_one + jnp.sum(norm_one_grad * normed_one, axis=(0, 1))
        grad_shift_one = grad_shift_one + jnp.sum(norm_one_grad, axis=(0, 1))
        grad_list.append(
            grad_resid + norm_backward(norm_one_grad, normed_one, inverse_one, gain_one)
        )
    grad_qkv, grad_qv, grad_proj, grad_fc, grad_fc_bias, grad_out = lax.psum(
        (grad_qkv, grad_qv, grad_proj, grad_fc, grad_fc_bias, grad_out), "dp"
    )
    grad_gain_one, grad_shift_one, grad_proj_bias, grad_gain_two, grad_shift_two, grad_out_bias = (
        lax.psum(
            (
                grad_gain_one,
                grad_shift_one,
                grad_proj_bias,
                grad_gain_two,
                grad_shift_two,
                grad_out_bias,
            ),
            ("dp", "tensor"),
        )
    )
    outputs = jnp.stack(output_list, axis=0)
    grad_inputs = jnp.stack(grad_list, axis=0)
    return (
        outputs,
        grad_inputs,
        grad_gain_one,
        grad_shift_one,
        grad_qkv.reshape(model_width, 3, local_width),
        grad_qv,
        grad_proj,
        grad_proj_bias,
        grad_gain_two,
        grad_shift_two,
        grad_fc,
        grad_fc_bias,
        grad_out,
        grad_out_bias,
    )


def solution(mesh):
    return jax.shard_map(
        body,
        mesh=mesh,
        in_specs=(
            P(None, "dp", "tensor", None),
            P(None, "dp", "tensor", None),
            P(None, "dp"),
            P(),
            P(),
            P(None, None, "tensor"),
            P(None, "tensor"),
            P("tensor", None),
            P(),
            P(),
            P(),
            P(None, "tensor"),
            P("tensor"),
            P("tensor", None),
            P(),
        ),
        out_specs=(
            P(None, "dp", "tensor", None),
            P(None, "dp", "tensor", None),
            P(),
            P(),
            P(None, None, "tensor"),
            P(None, "tensor"),
            P("tensor", None),
            P(),
            P(),
            P(),
            P(None, "tensor"),
            P("tensor"),
            P("tensor", None),
            P(),
        ),
        check_vma=False,
    )
```

profile of v0, /device:TPU:0, one launch (start us, length us, event | category | flops | bytes accessed | tf_op | source)
XLA Modules:
  0.0 948.5 jit_solution(637601627696089566)
XLA Ops:
  20.2 21.7 %all-gather.13.cloned.1.call-done = bf16[1,1024,768]{2,1,0:T(8,128)(2,1)} async-done(((bf16[1,512,768]{2,1,0:T(8,128)(2,1)}), bf16[1,1024,768]{2,1,0:T(8,128)(2,1)}) %all-gather.13.cloned.1.call-update) | async-done | bytes 1572880 | tf_op jit(solution)/shard_map/all_gather | solution.py:90
  51.8 19.4 %all-gather.9.cloned.1.call-done = bf16[1,1024,768]{2,1,0:T(8,128)(2,1)} async-done(((bf16[1,512,768]{2,1,0:T(8,128)(2,1)}), bf16[1,1024,768]{2,1,0:T(8,128)(2,1)}) %all-gather.9.cloned.1.call-update) | async-done | bytes 1572880 | tf_op jit(solution)/shard_map/all_gather | solution.py:90
  131.0 20.7 %reduce-scatter.9.cloned.1.call-done = f32[1,512,768]{2,1,0:T(8,128)} async-done(((f32[1,1024,768]{2,1,0:T(8,128)}), f32[1,512,768]{2,1,0:T(8,128)}) %reduce-scatter.9.cloned.1.call-update) | async-done | bytes 1572880 | tf_op jit(solution)/shard_map/reduce_scatter | solution.py:140
  151.6 46.1 %reduce-scatter.13.cloned.1.call-done = f32[1,512,768]{2,1,0:T(8,128)} async-done(((f32[1,1024,768]{2,1,0:T(8,128)}), f32[1,512,768]{2,1,0:T(8,128)}) %reduce-scatter.13.cloned.1.call-update) | async-done | bytes 1572880 | tf_op jit(solution)/shard_map/reduce_scatter | solution.py:140
  209.0 21.7 %all-gather.15.cloned.1.call-done = bf16[1,1024,768]{2,1,0:T(8,128)(2,1)} async-done(((bf16[1,512,768]{2,1,0:T(8,128)(2,1)}), bf16[1,1024,768]{2,1,0:T(8,128)(2,1)}) %all-gather.15.cloned.1.call-update) | async-done | bytes 1572880 | tf_op jit(solution)/shard_map/all_gather | solution.py:144
  243.0 16.8 %all-gather.11.cloned.1.call-done = bf16[1,1024,768]{2,1,0:T(8,128)(2,1)} async-done(((bf16[1,512,768]{2,1,0:T(8,128)(2,1)}), bf16[1,1024,768]{2,1,0:T(8,128)(2,1)}) %all-gather.11.cloned.1.call-update) | async-done | bytes 1572880 | tf_op jit(solution)/shard_map/all_gather | solution.py:144
  272.5 16.8 %all-gather.21.cloned.1.call-done = bf16[1,1024,768]{2,1,0:T(8,128)(2,1)} async-done(((bf16[1,512,768]{2,1,0:T(8,128)(2,1)}), bf16[1,1024,768]{2,1,0:T(8,128)(2,1)}) %all-gather.21.cloned.1.call-update) | async-done | bytes 1572880 | tf_op jit(solution)/shard_map/all_gather | solution.py:163
  304.2 14.4 %all-gather.17.cloned.1.call-done = bf16[1,1024,768]{2,1,0:T(8,128)(2,1)} async-done(((bf16[1,512,768]{2,1,0:T(8,128)(2,1)}), bf16[1,1024,768]{2,1,0:T(8,128)(2,1)}) %all-gather.17.cloned.1.call-update) | async-done | bytes 1572880 | tf_op jit(solution)/shard_map/all_gather | solution.py:163
  334.2 13.4 %reduce-scatter.15.cloned.1.call-done = bf16[1,512,768]{2,1,0:T(8,128)(2,1)} async-done(((bf16[1,1024,768]{2,1,0:T(8,128)(2,1)}), bf16[1,512,768]{2,1,0:T(8,128)(2,1)}) %reduce-scatter.15.cloned.1.call-update) | async-done | bytes 786448 | tf_op jit(solution)/shard_map/reduce_scatter | solution.py:154
  347.5 28.3 %reduce-scatter.11.cloned.1.call-done = bf16[1,512,768]{2,1,0:T(8,128)(2,1)} async-done(((bf16[1,1024,768]{2,1,0:T(8,128)(2,1)}), bf16[1,512,768]{2,1,0:T(8,128)(2,1)}) %reduce-scatter.11.cloned.1.call-update) | async-done | bytes 786448 | tf_op jit(solution)/shard_map/reduce_scatter | solution.py:154
  375.8 46.2 %reduce-scatter.21.cloned.1.call-done = f32[1,512,768]{2,1,0:T(8,128)} async-done(((f32[1,1024,768]{2,1,0:T(8,128)}), f32[1,512,768]{2,1,0:T(8,128)}) %reduce-scatter.21.cloned.1.call-update) | async-done | bytes 1572880 | tf_op jit(solution)/shard_map/reduce_scatter | solution.py:178
  422.0 46.1 %reduce-scatter.17.cloned.1.call-done = f32[1,512,768]{2,1,0:T(8,128)} async-done(((f32[1,1024,768]{2,1,0:T(8,128)}), f32[1,512,768]{2,1,0:T(8,128)}) %reduce-scatter.17.cloned.1.call-update) | async-done | bytes 1572880 | tf_op jit(solution)/shard_map/reduce_scatter | solution.py:178
  486.8 9.5 fusion.96
  497.8 10.1 %all-gather.23.cloned.1.call-done = bf16[1,1024,768]{2,1,0:T(8,128)(2,1)} async-done(((bf16[1,512,768]{2,1,0:T(8,128)(2,1)}), bf16[1,1024,768]{2,1,0:T(8,128)(2,1)}) %all-gather.23.cloned.1.call-update) | async-done | bytes 1572880 | tf_op jit(solution)/shard_map/all_gather | solution.py:185
  516.1 10.9 %multiply_reduce_fusion = (f32[6,512]{1,0:T(8,128)S(1)}, f32[6,512,1024]{2,1,0:T(8,128)}) fusion(f32[6,512,1024]{2,1,0:T(8,128)} %copy-done.5, f32[6,512]{1,0:T(8,128)S(1)} %log_add_fusion, bf16[1,1024,3,6,64]{1,4,3,2,0:T(8,128)(2,1)S(1)} %bitcast.378, bf16[1,1024,6,64]{1,3,2,0:T(8,128)(2,1)S(1)} %bitcast.386), kind=kOutput, calls=%fused_computation.1 | convolution fusion | flops 412087296 | bytes 26374144 | tf_op jit(solution)/shard_map/sqhe,skhe->shqk/dot_general | solution.py:203
  527.0 9.5 multiply_convert_fusion
  544.6 9.1 multiply_convert_fusion.1
  571.9 10.6 %multiply_reduce_fusion.2 = (f32[6,512]{1,0:T(8,128)S(1)}, f32[6,512,1024]{2,1,0:T(8,128)}) fusion(f32[6,512,1024]{2,1,0:T(8,128)} %copy-done.4, f32[6,512]{1,0:T(8,128)S(1)} %log_add_fusion.2, bf16[1,1024,3,6,64]{1,4,3,2,0:T(8,128)(2,1)S(1)} %bitcast.369, bf16[1,1024,6,64]{1,3,2,0:T(8,128)(2,1)S(1)} %bitcast.389), kind=kOutput, calls=%fused_computation.7 | convolution fusion | flops 412087296 | bytes 26374144 | tf_op jit(solution)/shard_map/sqhe,skhe->shqk/dot_general | solution.py:203
  582.5 10.3 %multiply_convert_fusion.2 = bf16[6,512,1024]{2,1,0:T(8,128)(2,1)S(1)} fusion(f32[6,512,1024]{2,1,0:T(8,128)} %get-tuple-element.120, f32[6,512,1024]{2,1,0:T(8,128)} %copy-done.4, f32[6,512]{1,0:T(8,128)S(1)} %get-tuple-element.119, f32[6,512]{1,0:T(8,128)S(1)} %log_add_fusion.2), kind=kLoop, calls=%fused_computation.6 | loop fusion | flops 12582912 | bytes 31481856 | tf_op jit(solution)/shard_map/convert_element_type | solution.py:207
  600.9 9.0 multiply_convert_fusion.3
  638.2 10.5 %convolution_add_fusion.1 = f32[1536,768]{1,0:T(8,128)} fusion(f32[1536,768]{1,0:T(8,128)} %fusion.96, bf16[1,1024,768]{2,1,0:T(8,128)(2,1)S(1)} %copy-done.77, f32[1024,1536]{1,0:T(8,128)} %copy-done.88, f32[1536]{0:T(1024)S(1)} %copy-done.82), kind=kOutput, calls=%fused_computation.71 | convolution fusion | flops 2432827392 | bytes 17307648 | tf_op jit(solution)/shard_map/srf,srd->fd/dot_general | solution.py:164
  669.6 66.0 %all-reduce.1 = (f32[2,384]{1,0:T(2,128)}, f32[1536]{0:T(1024)}) all-reduce(f32[2,384]{1,0:T(2,128)S(1)} %maximum_add_fusion, f32[1536]{0:T(1024)S(1)} %add.419), channel_id=1, replica_groups=mesh['dp'=16,'tensor'=2] {'dp'}, use_global_device_ids=true, to_apply=%region_45.46 | all-reduce | flops 2304 | bytes 18432 | tf_op jit(solution)/shard_map/psum | solution.py:246
  738.5 38.8 %all-reduce = (f32[768]{0:T(1024)}, f32[768]{0:T(1024)}, f32[768]{0:T(1024)}, f32[768]{0:T(1024)}, f32[768]{0:T(1024)}, /*index=5*/f32[768]{0:T(1024)}) all-reduce(f32[768]{0:T(1024)S(1)} %add.410, f32[768]{0:T(1024)S(1)} %add.411, f32[768]{0:T(1024)S(1)} %add.415, ...), channel_id=1, replica_groups=mesh['dp'=16,'tensor'=2] {'dp','tensor'}, use_global_device_ids=true, to_apply=%region_38.39 | all-reduce | flops 4608 | bytes 36864 | tf_op jit(solution)/shard_map/psum | solution.py:250
  781.9 144.5 %all-reduce.5.cloned.1.call-done = (f32[768,3,384]{0,2,1:T(8,128)}, f32[384,768]{1,0:T(8,128)}, f32[768,1536]{1,0:T(8,128)}, f32[1536,768]{1,0:T(8,128)}) async-done(((f32[768,3,384]{0,2,1:T(8,128)}, f32[384,768]{1,0:T(8,128)}, f32[768,1536]{1,0:T(8,128)}, f32[1536,768]{1,0:T(8,128)}), (f32[768,3,384]{0,2,1:T(8,128)}, f32[384,768]{1,0:T(8,128)}, f32[768,1536]{1,0:T(8,128)}, ...) | async-done | bytes 14155792 | tf_op jit(solution)/shard_map/psum | solution.py:246
  (360 shorter events, 282.5 us)
Async XLA Ops:
  7.2 230.8 %copy-start = (bf16[1536,768]{1,0:T(8,128)(2,1)S(1)}, bf16[1536,768]{1,0:T(8,128)(2,1)}, u32[]{:S(2)}) copy-start(bf16[1536,768]{1,0:T(8,128)(2,1)} %param.28) | copy-start | bytes 7077892
  7.2 34.6 %all-gather.13.cloned.1.call-start = ((), (), s32[]{:S(2)}) async-start(), calls=%async_computation.12 | async-start | bytes 2359296 | tf_op jit(solution)/shard_map/all_gather | solution.py:90
  11.8 59.4 %all-gather.9.cloned.1.call-start = ((), (), s32[]{:S(2)}) async-start(), calls=%async_computation.8 | async-start | bytes 2359296 | tf_op jit(solution)/shard_map/all_gather | solution.py:90
  12.6 139.1 %reduce-scatter.9.cloned.1.call-start = ((), (), s32[]{:S(2)}) async-start(), calls=%async_computation.9 | async-start | bytes 4718592 | tf_op jit(solution)/shard_map/reduce_scatter | solution.py:140
  108.1 89.6 %reduce-scatter.13.cloned.1.call-start = ((), (), s32[]{:S(2)}) async-start(), calls=%async_computation.13 | async-start | bytes 4718592 | tf_op jit(solution)/shard_map/reduce_scatter | solution.py:140
  130.5 100.1 %all-gather.15.cloned.1.call-start = ((), (), s32[]{:S(2)}) async-start(), calls=%async_computation.14 | async-start | bytes 2359296 | tf_op jit(solution)/shard_map/all_gather | solution.py:144
  203.3 56.6 %all-gather.11.cloned.1.call-start = ((), (), s32[]{:S(2)}) async-start(), calls=%async_computation.10 | async-start | bytes 2359296 | tf_op jit(solution)/shard_map/all_gather | solution.py:144
  203.9 85.4 %all-gather.21.cloned.1.call-start = ((), (), s32[]{:S(2)}) async-start(), calls=%async_computation.20 | async-start | bytes 2359296 | tf_op jit(solution)/shard_map/all_gather | solution.py:163
  208.2 110.4 %all-gather.17.cloned.1.call-start = ((), (), s32[]{:S(2)}) async-start(), calls=%async_computation.16 | async-start | bytes 2359296 | tf_op jit(solution)/shard_map/all_gather | solution.py:163
  208.9 138.6 %reduce-scatter.15.cloned.1.call-start = ((), (), s32[]{:S(2)}) async-start(), calls=%async_computation.15 | async-start | bytes 2359296 | tf_op jit(solution)/shard_map/reduce_scatter | solution.py:154
  243.0 132.8 %reduce-scatter.11.cloned.1.call-start = ((), (), s32[]{:S(2)}) async-start(), calls=%async_computation.11 | async-start | bytes 2359296 | tf_op jit(solution)/shard_map/reduce_scatter | solution.py:154
  272.2 149.8 %reduce-scatter.21.cloned.1.call-start = ((), (), s32[]{:S(2)}) async-start(), calls=%async_computation.21 | async-start | bytes 4718592 | tf_op jit(solution)/shard_map/reduce_scatter | solution.py:178
  304.1 164.1 %reduce-scatter.17.cloned.1.call-start = ((), (), s32[]{:S(2)}) async-start(), calls=%async_computation.17 | async-start | bytes 4718592 | tf_op jit(solution)/shard_map/reduce_scatter | solution.py:178
  333.4 134.8 %copy-start.10 = (f32[1,512,768]{2,1,0:T(8,128)S(1)}, f32[1,512,768]{2,1,0:T(8,128)}, u32[]{:S(2)}) copy-start(f32[1,512,768]{2,1,0:T(8,128)} %copy-done.9) | copy-start | bytes 4718596
  333.4 134.8 %copy-start.69 = (f32[768]{0:T(1024)S(1)}, f32[768]{0:T(1024)}, u32[]{:S(2)}) copy-start(f32[768]{0:T(1024)} %param.29) | copy-start | bytes 9220
  333.4 174.5 %all-gather.23.cloned.1.call-start = ((), (), s32[]{:S(2)}) async-start(), calls=%async_computation.22 | async-start | bytes 2359296 | tf_op jit(solution)/shard_map/all_gather | solution.py:185
  480.5 89.0 %all-gather.19.cloned.1.call-start = ((), (), s32[]{:S(2)}) async-start(), calls=%async_computation.18 | async-start | bytes 2359296 | tf_op jit(solution)/shard_map/all_gather | solution.py:185
  497.4 238.2 %reduce-scatter.23.cloned.1.call-start = ((), (), s32[]{:S(2)}) async-start(), calls=%async_computation.23 | async-start | bytes 2359296 | tf_op jit(solution)/shard_map/reduce_scatter | solution.py:238
  569.4 166.2 %reduce-scatter.19.cloned.1.call-start = ((), (), s32[]{:S(2)}) async-start(), calls=%async_computation.19 | async-start | bytes 2359296 | tf_op jit(solution)/shard_map/reduce_scatter | solution.py:238
  631.1 295.3 %all-reduce.5.cloned.1.call-start = ((), (), s32[]{:S(2)}) async-start(), calls=%async_computation.24 | async-start | bytes 28311552 | tf_op jit(solution)/shard_map/psum | solution.py:246
  665.4 70.2 %copy-start.8 = (bf16[2,1,512,768]{3,2,1,0:T(8,128)(2,1)S(1)}, bf16[2,1,512,768]{3,2,1,0:T(8,128)(2,1)}, u32[]{:S(2)}) copy-start(bf16[2,1,512,768]{3,2,1,0:T(8,128)(2,1)} %param.15) | copy-start | bytes 4718596
  665.4 70.2 %copy-start.46 = (f32[512]{0:T(512)S(1)}, f32[512]{0:T(512)}, u32[]{:S(2)}) copy-start(f32[512]{0:T(512)} %copy-done.45) | copy-start | bytes 6148
  665.4 70.2 %copy-start.48 = (f32[512]{0:T(512)S(1)}, f32[512]{0:T(512)}, u32[]{:S(2)}) copy-start(f32[512]{0:T(512)} %copy-done.47) | copy-start | bytes 6148
  665.4 70.2 %copy-start.51 = (f32[768]{0:T(1024)S(1)}, f32[768]{0:T(1024)}, u32[]{:S(2)}) copy-start(f32[768]{0:T(1024)} %param.18) | copy-start | bytes 9220
  (93 other events, 752.0 us)
Sparse Core Ops, SparseCore 0:
  11.9 29.8 all-gather.12
  44.0 27.2 all-gather.8
  108.3 43.3 reduce-scatter.8
  154.4 43.3 reduce-scatter.12
  203.4 27.2 all-gather.14
  232.6 27.2 all-gather.10
  262.0 27.2 all-gather.20
  291.3 27.2 all-gather.16
  321.4 26.0 reduce-scatter.14
  349.7 26.0 reduce-scatter.10
  378.7 43.3 reduce-scatter.20
  424.8 43.3 reduce-scatter.16
  480.6 27.2 all-gather.22
  509.8 27.1 all-gather.18
  569.6 26.8 reduce-scatter.22
  631.2 26.7 reduce-scatter.18
  664.7 261.6 all-reduce.4
where the time goes:
time: 959 us; the launch traced here: 949 us
  waiting for transfers between devices  468 us (49%)
  matrix products  212 us (22%)
  blocking collectives  105 us (11%)
  other arithmetic  90.5 us (9%)
  local copies, waits for them, and re-layouts  55.4 us (6%)
  between operations  15.7 us (2%)
    psum x1, waiting for transfers between devices, body(): lax.psum((grad_qkv, grad_qv, grad_proj, grad_fc, grad_fc_bias, grad_out),...  144 us
    reduce_scatter x2, waiting for transfers between devices, body(): lax.psum_scatter(norm_two_part, 'tensor', scatter_dimension=1, tiled=True)  92.3 us
    reduce_scatter x2, waiting for transfers between devices, body(): lax.psum_scatter(attn_part, 'tensor', scatter_dimension=1, tiled=True)  66.8 us
    psum x1, blocking collectives, body(): lax.psum((grad_qkv, grad_qv, grad_proj, grad_fc, grad_fc_bias, grad_out),...  66 us
    reduce_scatter x2, waiting for transfers between devices, body(): lax.psum_scatter(mlp_part.astype(jnp.bfloat16), 'tensor', scatter_dimensi...  41.7 us
    all_gather x2, waiting for transfers between devices, body(): full_one = lax.all_gather(local_one, 'tensor', axis=1, tiled=True)  41.1 us
    psum x1, blocking collectives, body(): lax.psum((grad_gain_one, grad_shift_one, grad_proj_bias, grad_gain_two, g...  38.8 us
    all_gather x2, waiting for transfers between devices, body(): full_two = lax.all_gather(local_two, 'tensor', axis=1, tiled=True)  38.5 us
  transfers between devices with their start and end apart: 17, of which 14 were waited for; matrix products, arithmetic and copies ran while one was open for 29% of the time, Pallas kernels for 0%

commit v1 on v0

v1 whole, which is shorter than its diff:
```python
import functools

import jax
import jax.numpy as jnp
from jax import lax
from jax.experimental import pallas as pl
from jax.experimental.pallas import tpu as pltpu
from jax.sharding import PartitionSpec as P

F = jnp.float32
B = jnp.bfloat16
T = 1024
D = 768
HD = 64
HW = 384
FF = 3072
FH = 1536
CH = 512
RT = 256
QB = 256
NP = 6
EPS = 1e-05
SB = 48 ** (-0.5)
RC = 0.7978845608028654
CC = 0.044715


def nn(a, b):
    return lax.dot_general(a, b, (((1,), (0,)), ((), ())), preferred_element_type=F)


def nt(a, b):
    return lax.dot_general(a, b, (((1,), (1,)), ((), ())), preferred_element_type=F)


def tn(a, b):
    return lax.dot_general(a, b, (((0,), (0,)), ((), ())), preferred_element_type=F)


def rows_of(r):
    return pl.ds(pl.multiple_of(r * RT, RT), RT)


def norm(v):
    cen = v - jnp.mean(v, axis=-1, keepdims=True)
    inv = lax.rsqrt(jnp.mean(cen * cen, axis=-1, keepdims=True) + EPS)
    return cen * inv, inv


def norm_back(e, n, inv):
    return inv * (e - jnp.mean(e, axis=-1, keepdims=True) - n * jnp.mean(e * n, axis=-1, keepdims=True))


def gelu_pair(u):
    u2 = u * u
    t = jnp.tanh(RC * (u + CC * u2 * u))
    hp = 0.5 * (1.0 + t)
    return u * hp, hp + (0.5 * RC) * u * (1.0 - t * t) * (1.0 + (3.0 * CC) * u2)


def phase_qkv(x, a1, wqkv, bqkv, g1, s1, qkv):
    def row(r, _):
        rr = rows_of(r)
        n1, _inv = norm(x[rr, :].astype(F))
        a = (n1 * g1[...] + s1[...]).astype(B)
        a1[rr, :] = a
        for t in range(3):
            v = nn(a, wqkv[:, t * D : (t + 1) * D]) + bqkv[:, t * D : (t + 1) * D]
            if t == 0:
                v = v * 0.125
            qkv[rr, t * D : (t + 1) * D] = v.astype(B)
        return 0

    lax.fori_loop(0, T // RT, row, 0)


def pair_attention(hp, n, qkv, o, lse):
    off = pl.multiple_of(hp * 128, 128)
    lane = lax.broadcasted_iota(jnp.int32, (QB, 128), 1)
    for qb in range(T // QB):
        ext = (qb + 1) * QB
        q2 = qkv[pl.ds(qb * QB, QB), pl.ds(off, 128)]
        k2 = qkv[pl.ds(0, ext), pl.ds(D + off, 128)]
        v2 = qkv[pl.ds(0, ext), pl.ds(2 * D + off, 128)]
        key = lax.broadcasted_iota(jnp.int32, (ext, QB), 0)
        qi = lax.broadcasted_iota(jnp.int32, (ext, QB), 1) + qb * QB
        bound = jnp.minimum(qi + 1, n)
        outs = []
        for h in range(2):
            qm = jnp.where((lane // HD) == h, q2, jnp.zeros_like(q2))
            s = jnp.where(key < bound, nt(k2, qm), -1e30)
            m = jnp.max(s, axis=0, keepdims=True)
            e = jnp.exp(s - m)
            l = jnp.sum(e, axis=0, keepdims=True)
            pb = (e * (1.0 / l)).astype(B)
            outs.append(tn(pb, v2))
            lse[pl.ds(hp * 2 + h, 1), pl.ds(qb * QB, QB)] = m + jnp.log(l)
        o[pl.ds(qb * QB, QB), pl.ds(off, 128)] = jnp.where(lane < HD, outs[0], outs[1]).astype(B)


def pair_backward(hp, n, qkv, do, o, lse, dk_s, dv_s, dq_s):
    off = pl.multiple_of(hp * 128, 128)
    lane = lax.broadcasted_iota(jnp.int32, (QB, 128), 1)
    for qb in reversed(range(T // QB)):
        ext = (qb + 1) * QB
        rq = pl.ds(qb * QB, QB)
        q2 = qkv[rq, pl.ds(off, 128)]
        k2 = qkv[pl.ds(0, ext), pl.ds(D + off, 128)]
        v2 = qkv[pl.ds(0, ext), pl.ds(2 * D + off, 128)]
        do2 = do[rq, pl.ds(off, 128)]
        o2 = o[rq, pl.ds(off, 128)]
        prod = (do2.astype(F) * o2.astype(F)).T
        key = lax.broadcasted_iota(jnp.int32, (ext, QB), 0)
        qi = lax.broadcasted_iota(jnp.int32, (ext, QB), 1) + qb * QB
        bound = jnp.minimum(qi + 1, n)
        dqs, dks, dvs = [], [], []
        for h in range(2):
            hm = (lane // HD) == h
            qm = jnp.where(hm, q2, jnp.zeros_like(q2))
            dm = jnp.where(hm, do2, jnp.zeros_like(do2))
            dd = jnp.sum(prod[h * HD : (h + 1) * HD], axis=0, keepdims=True)
            ls = lse[pl.ds(hp * 2 + h, 1), rq]
            p = jnp.where(key < bound, jnp.exp(nt(k2, qm) - ls), 0.0)
            ds = (p * (nt(v2, dm) - dd)).astype(B)
            dqs.append(tn(k2, ds).T)
            dks.append(nn(ds, qm))
            dvs.append(nn(p.astype(B), dm))
        dq_s[rq, :] = (jnp.where(lane < HD, dqs[0], dqs[1]) * 0.125).astype(B)
        dk = dks[0] + dks[1]
        dv = dvs[0] + dvs[1]
        if qb == T // QB - 1:
            dk_s[...] = dk
            dv_s[...] = dv
        else:
            dk_s[pl.ds(0, ext), :] += dk
            dv_s[pl.ds(0, ext), :] += dv
    qkv[:, pl.ds(off, 128)] = dq_s[...]
    qkv[:, pl.ds(D + off, 128)] = dk_s[...].astype(B)
    qkv[:, pl.ds(2 * D + off, 128)] = dv_s[...].astype(B)


def phase_mid(n, x, c, o, wproj, bproj, g2, s2, r1, a2, dm, small):
    def row(r, ob):
        rr = rows_of(r)
        v = x[rr, :].astype(F) + SB * (nn(o[rr, :], wproj[...]) + bproj[...])
        r1[rr, :] = v
        n2, _inv = norm(v)
        a2[rr, :] = (n2 * g2[...] + s2[...]).astype(B)
        ids = lax.broadcasted_iota(jnp.int32, (RT, 1), 0) + r * RT
        cs = SB * (c[rr, :].astype(F) * (ids < n).astype(F))
        dm[rr, :] = cs.astype(B)
        return ob + jnp.sum(cs, axis=0, keepdims=True)

    small[5:6, :] = lax.fori_loop(0, T // RT, row, jnp.zeros((1, D), F))


def mlp_chunk(k, w1, w2, bias, a2, dm, m, da2, hs, dus, gfc, gout, gb):
    tot = jnp.zeros((1, CH), F)
    for r in range(T // RT):
        rr = pl.ds(r * RT, RT)
        u = nn(a2[rr, :], w1[...]) + bias
        h, sl = gelu_pair(u)
        hb = h.astype(B)
        hs[rr, :] = hb
        du = (nt(dm[rr, :], w2[...]) * sl).astype(B)
        dus[rr, :] = du
        m[rr, :] += nn(hb, w2[...])
        da2[rr, :] += nt(du, w1[...])
        tot = tot + jnp.sum(du.astype(F), axis=0, keepdims=True)
    gb[...] = tot
    gout[...] = tn(hs[...], dm[...]).astype(B)
    gfc[...] = tn(a2[...], dus[...]).astype(B)


def phase_back(n, c, r1, m, da2, bout, g2, wproj, dattn, do, out, small):
    def row(r, acc):
        rr = rows_of(r)
        v = r1[rr, :]
        out[rr, :] = (v + SB * (m[rr, :] + bout[...])).astype(B)
        n2, inv = norm(v)
        g = da2[rr, :]
        ids = lax.broadcasted_iota(jnp.int32, (RT, 1), 0) + r * RT
        dr = c[rr, :].astype(F) * (ids < n).astype(F) + norm_back(g * g2[...], n2, inv)
        da2[rr, :] = dr
        sr = SB * dr
        sb = sr.astype(B)
        dattn[rr, :] = sb
        do[rr, :] = nt(sb, wproj[...]).astype(B)
        total = lambda w: jnp.sum(w, axis=0, keepdims=True)
        return acc[0] + total(g * n2), acc[1] + total(g), acc[2] + total(sr)

    z = jnp.zeros((1, D), F)
    a, b, p = lax.fori_loop(0, T // RT, row, (z, z, z))
    small[2:3, :] = p
    small[3:4, :] = a
    small[4:5, :] = b


def phase_end(x, qkv, wqkv, g1, dr1, gin, small):
    def row(r, acc):
        rr = rows_of(r)
        g = nt(qkv[rr, :], wqkv[...])
        n1, inv = norm(x[rr, :].astype(F))
        gin[rr, :] = (dr1[rr, :] + norm_back(g * g1[...], n1, inv)).astype(B)
        total = lambda w: jnp.sum(w, axis=0, keepdims=True)
        return acc[0] + total(g * n1), acc[1] + total(g)

    z = jnp.zeros((1, D), F)
    a, b = lax.fori_loop(0, T // RT, row, (z, z))
    small[0:1, :] = a
    small[1:2, :] = b


def kernel(lens, x, c, g1, s1, wqkv, bqkv, wproj, bproj, g2, s2, wfc, bfc, wout, bout,
           out, gin, gqkv, gproj, gfc, gout, small, gqv, gfcb,
           a1, qkv, o, lse, r1, a2, dm, m, da2, hs, dus, do, dk_s, dv_s, dq_s):
    n = lens[0]
    phase_qkv(x, a1, wqkv, bqkv, g1, s1, qkv)

    def fwd(hp, _):
        pair_attention(hp, n, qkv, o, lse)
        return 0

    lax.fori_loop(0, NP, fwd, 0)
    phase_mid(n, x, c, o, wproj, bproj, g2, s2, r1, a2, dm, small)
    m[...] = jnp.zeros_like(m)
    da2[...] = jnp.zeros_like(da2)

    def chunk(k, _):
        hc = pl.ds(pl.multiple_of(k * CH, CH), CH)
        mlp_chunk(k, wfc.at[k], wout.at[hc], bfc[k], a2, dm, m, da2, hs, dus, gfc.at[k], gout.at[hc], gfcb.at[k])
        return 0

    lax.fori_loop(0, FF // CH, chunk, 0)
    phase_back(n, c, r1, m, da2, bout, g2, wproj, dm, do, out, small)
    gproj[...] = tn(o[...], dm[...]).astype(B)

    def bwd(hp, _):
        pair_backward(hp, n, qkv, do, o, lse, dk_s, dv_s, dq_s)
        off = pl.multiple_of(hp * 128, 128)
        for t in range(3):
            d = qkv[:, pl.ds(t * D + off, 128)]
            gqkv[hp, :, t * 128 : (t + 1) * 128] = tn(a1[...], d).astype(B)
            if t != 1:
                gqv[t // 2 : t // 2 + 1, pl.ds(off, 128)] = jnp.sum(d.astype(F), axis=0, keepdims=True)
        return 0

    lax.fori_loop(0, NP, bwd, 0)
    phase_end(x, qkv, wqkv, g1, da2, gin, small)
    small[6:8, :] = jnp.zeros((2, D), F)


def local_call(*args):
    V = pl.BlockSpec(memory_space=pltpu.VMEM)
    S = pl.BlockSpec(memory_space=pltpu.SMEM)
    sd = jax.ShapeDtypeStruct
    outs = (sd((T, D), B), sd((T, D), B), sd((NP, D, HW), B), sd((D, D), B), sd((FF // CH, D, CH), B),
            sd((FF, D), B), sd((8, D), F), sd((2, D), F), sd((FF // CH, 1, CH), F))
    vm = pltpu.VMEM
    return pl.pallas_call(
        kernel,
        out_shape=outs,
        in_specs=[S] + [V] * 14,
        out_specs=(V, V, V, V, V, V, V, V, V),
        scratch_shapes=[
            vm((T, D), B), vm((T, 3 * D), B), vm((T, D), B), vm((16, T), F), vm((T, D), F), vm((T, D), B),
            vm((T, D), B), vm((T, D), F), vm((T, D), F), vm((T, CH), B), vm((T, CH), B), vm((T, D), B),
            vm((T, 128), F), vm((T, 128), F), vm((T, 128), B),
        ],
        compiler_params=pltpu.CompilerParams(vmem_limit_bytes=62 * 2**20),
    )(*args)


def body(inputs, cotangent, lengths, gain_one, shift_one, qkv_weight, qv_bias, proj_weight, proj_bias, gain_two,
         shift_two, fc_weight, fc_bias, out_weight, out_bias):
    ti = lax.axis_index("tensor")
    swap = lambda v: lax.ppermute(v, "tensor", [(0, 1), (1, 0)])
    pick = lambda v, i: lax.dynamic_index_in_dim(v, i, 0, keepdims=False)

    def whole(v):
        mine = pick(v, ti)[0]
        theirs = swap(pick(v, 1 - ti)[0])
        return jnp.where(ti == 0, jnp.concatenate([mine, theirs]), jnp.concatenate([theirs, mine]))

    x = whole(inputs)
    c = whole(cotangent)
    n = pick(lengths, ti)
    wq = jnp.transpose(qkv_weight, (1, 0, 2))
    wq2 = jnp.stack([wq, swap(wq)], axis=1)
    wqkv = jnp.transpose(wq2, (2, 0, 1, 3)).reshape(D, 3 * D)
    bq = jnp.stack([qv_bias, swap(qv_bias)], axis=1).reshape(2, D)
    bqkv = jnp.concatenate([bq[0], jnp.zeros((D,), F), bq[1]]).reshape(1, 3 * D)
    wproj = jnp.concatenate([proj_weight, swap(proj_weight)])
    chunks = lambda v: jnp.transpose(v.reshape(D, FH // CH, CH), (1, 0, 2))
    wfc = jnp.concatenate([chunks(fc_weight), chunks(swap(fc_weight))])
    bfc = jnp.concatenate([fc_bias, swap(fc_bias)]).reshape(FF // CH, 1, CH)
    wout = jnp.concatenate([out_weight, swap(out_weight)])
    row = lambda v: v.reshape(1, D)
    out, gin, gqkv, gproj, gfc, gout, small, gqv, gfcb = local_call(
        n, x, c, row(gain_one), row(shift_one), wqkv, bqkv, wproj, row(proj_bias), row(gain_two), row(shift_two),
        wfc, bfc, wout, row(out_bias))

    def spread(v):
        half = v.reshape(2, T // 2, D)
        mine = pick(half, ti)
        theirs = swap(pick(half, 1 - ti))
        return jnp.where(ti == 0, jnp.stack([mine, theirs]), jnp.stack([theirs, mine])).astype(F)[:, None]

    def total(v):
        k = v.shape[0] // 2
        return lax.psum(v[:k] + swap(v[k:]), "dp").astype(F)

    gqkv, gproj, gfc, gout = [total(v) for v in (gqkv, gproj, gfc, gout)]
    gqkv = jnp.transpose(gqkv.reshape(3, D, 3, 128), (1, 2, 0, 3)).reshape(D, 3, HW)
    gfc = jnp.transpose(gfc, (1, 0, 2)).reshape(D, FH)
    small = lax.psum(small, ("dp", "tensor"))
    side = jnp.concatenate([gqv.reshape(2, 2, HW), gfcb.reshape(2, 4, HW).transpose(1, 0, 2)])
    side = lax.psum(side[:, 0] + swap(side[:, 1]), "dp")
    return (spread(out), spread(gin), small[0], small[1], gqkv, side[:2], gproj, small[2], small[3], small[4], gfc,
            side[2:].reshape(FH), gout, small[5])


def solution(mesh):
    dp = P(None, "dp", "tensor", None)
    return jax.shard_map(
        body,
        mesh=mesh,
        in_specs=(dp, dp, P(None, "dp"), P(), P(), P(None, None, "tensor"), P(None, "tensor"), P("tensor", None), P(),
                  P(), P(), P(None, "tensor"), P("tensor"), P("tensor", None), P()),
        out_specs=(dp, dp, P(), P(), P(None, None, "tensor"), P(None, "tensor"), P("tensor", None), P(), P(), P(),
                   P(None, "tensor"), P("tensor"), P("tensor", None), P()),
        check_vma=False,
    )
```

time: 959 us -> 698 us (0.73)
  matrix products: 212 us -> 0 us
  waiting for transfers between devices: 468 us -> 326 us
  Pallas kernels: 0 us -> 123 us
  other arithmetic: 90.5 us -> 36.7 us
  blocking collectives: 105 us -> 125 us
  starting transfers between devices: 1.68 us -> 17.4 us
    ppermute x0 -> x15, waiting for transfers between devices: none -> 309 us  [body(): swap = lambda v: lax.ppermute(v, 'tensor', [(0, 1), (1, 0)])]
    dot_general x48 -> x0, matrix products: 212 us -> none  [the longest x4 33.6 us: body(): jnp.einsum('sqhe,skhe->shqk', grad_block, value_all, preferred_element_ty...]
    reduce_scatter x8 -> x0, waiting for transfers between devices: 201 us -> none  [the longest x2 92.3 us: body(): lax.psum_scatter(norm_two_part, 'tensor', scatter_dimension=1, tiled=True)]
    psum x1, waiting for transfers between devices: 144 us -> 16.6 us  [total(): return lax.psum(v[:k] + swap(v[k:]), 'dp').astype(F)]
    pallas_call x0 -> x1, Pallas kernels: none -> 123 us  [local_call(): pl.pallas_call(kernel, out_shape=outs, in_specs=[S] + [V] * 14, out_specs...]
    all_gather x8 -> x0, waiting for transfers between devices: 121 us -> none  [the longest x2 41.1 us: body(): full_one = lax.all_gather(local_one, 'tensor', axis=1, tiled=True)]
    convert_element_type x10 -> x4, other arithmetic: 47.6 us -> 8.72 us  [the longest x2 4.83 us: total(): return lax.psum(v[:k] + swap(v[k:]), 'dp').astype(F)]
    reduce_sum x14 -> x0, other arithmetic: 31.2 us -> none  [the longest x4 11.5 us: body(): row_total = jnp.sum(expd, axis=-1, keepdims=True)]
  transfers between devices with their start and end apart: 17 -> 16, of which waited for: 14 -> 5; matrix products, arithmetic and copies ran while one was open for 29% -> 9% of each run, Pallas kernels for 0% -> 0%
where the time goes in v1:
time: 698 us; the launch traced here: 697 us
  waiting for transfers between devices  326 us (47%)
  blocking collectives  125 us (18%)
  Pallas kernels  123 us (18%)
  local copies, waits for them, and re-layouts  54 us (8%)
  other arithmetic  36.7 us (5%)
  starting transfers between devices  17.4 us (2%)
  between operations  14.3 us (2%)
    ppermute x15, waiting for transfers between devices, body(): swap = lambda v: lax.ppermute(v, 'tensor', [(0, 1), (1, 0)])  309 us
    pallas_call x1, Pallas kernels, local_call(): pl.pallas_call(kernel, out_shape=outs, in_specs=[S] + [V] * 14, out_specs...  123 us
    psum x1, blocking collectives, body(): small = lax.psum(small, ('dp', 'tensor'))  65.7 us
    psum x1, blocking collectives, body(): side = lax.psum(side[:, 0] + swap(side[:, 1]), 'dp')  59.8 us
    ppermute x15, starting transfers between devices, body(): swap = lambda v: lax.ppermute(v, 'tensor', [(0, 1), (1, 0)])  17.4 us
    psum x1, waiting for transfers between devices, total(): return lax.psum(v[:k] + swap(v[k:]), 'dp').astype(F)  16.6 us
  transfers between devices with their start and end apart: 16, of which 5 were waited for; matrix products, arithmetic and copies ran while one was open for 9% of the time, Pallas kernels for 0%

profile of v1, /device:TPU:0, one launch (start us, length us, event | category | flops | bytes accessed | tf_op | source)
XLA Modules:
  0.0 697.1 jit_solution(14579122789920357808)
XLA Ops:
  7.3 4.4 copy.33
  11.7 2.9 collective-permute-start.5
  18.7 148.7 %collective-permute-done.3 = f32[2,384]{1,0:T(2,128)S(1)} collective-permute-done((f32[2,384]{1,0:T(2,128)S(1)}, f32[2,384]{1,0:T(2,128)S(1)}, u32[]{:S(2)}, u32[]{:S(2)}) %collective-permute-start.3) | collective-permute-done | bytes 3104 | tf_op jit(solution)/shard_map/ppermute | solution.py:277
  180.0 4.3 copy.34
  187.9 4.4 collective-permute-done
  192.3 3.1 maximum_select_fusion.x
  195.4 11.5 %collective-permute-done.1 = bf16[512,768]{1,0:T(8,128)(2,1)} collective-permute-done((bf16[512,768]{1,0:T(8,128)(2,1)}, bf16[512,768]{1,0:T(8,128)(2,1)}, u32[]{:S(2)}, u32[]{:S(2)}) %collective-permute-start.1) | collective-permute-done | bytes 786464 | tf_op jit(solution)/shard_map/ppermute | solution.py:277
  206.9 3.1 maximum_select_fusion.1.c
  211.8 3.6 copy.32
  215.5 4.0 reshape.223.wqkv
  219.5 4.4 copy.36
  223.9 4.3 pad_maximum_fusion.wfc
  228.2 4.9 pad_maximum_fusion.1.wout
  233.0 123.3 %shard_map.254 = (bf16[1024,768]{1,0:T(8,128)(2,1)}, bf16[1024,768]{1,0:T(8,128)(2,1)}, bf16[6,768,384]{2,1,0:T(8,128)(2,1)}, bf16[768,768]{1,0:T(8,128)(2,1)}, ...) custom-call(s32[1]{0:T(128)} %bitcast.lens, ...), custom_call_target="tpu_custom_call" | custom-call | tf_op jit(solution)/shard_map/pallas_call | solution.py:260
  356.3 3.4 slice.77
  367.1 144.8 %collective-permute-done.12 = bf16[384,768]{1,0:T(8,128)(2,1)S(1)} collective-permute-done((bf16[384,768]{1,0:T(8,128)(2,1)S(1)}, bf16[384,768]{1,0:T(8,128)(2,1)S(1)}, u32[]{:S(2)}, u32[]{:S(2)}) %collective-permute-start.12) | collective-permute-done | bytes 589856 | tf_op jit(solution)/shard_map/ppermute | solution.py:277
  515.3 2.6 add_bitcast_fusion
  520.4 4.0 slice_add_fusion
  530.3 65.7 %psum.42 = f32[8,768]{1,0:T(8,128)S(1)} all-reduce(f32[8,768]{1,0:T(8,128)S(1)} %copy-done.11), channel_id=1, replica_groups=mesh['dp'=16,'tensor'=2] {'dp','tensor'}, use_global_device_ids=true, to_apply=%region_0.1 | all-reduce | flops 6144 | bytes 49152 | tf_op jit(solution)/shard_map/psum | solution.py:316
  596.6 59.8 %psum.44 = f32[6,384]{1,0:T(8,128)S(1)} all-reduce(f32[6,384]{1,0:T(8,128)S(1)} %fusion.4), channel_id=1, replica_groups=mesh['dp'=16,'tensor'=2] {'dp'}, use_global_device_ids=true, to_apply=%region_2.3 | all-reduce | flops 2304 | bytes 18432 | tf_op jit(solution)/shard_map/psum | solution.py:318
  661.5 16.6 %all-reduce.3.cloned.1.call-done = (bf16[768,3,384]{0,2,1:T(8,128)(2,1)}, bf16[768,1536]{0,1:T(8,128)(2,1)}, bf16[384,768]{1,0:T(8,128)(2,1)}, bf16[1536,768]{1,0:T(8,128)(2,1)}) async-done(((bf16[768,3,384]{0,2,1:T(8,128)(2,1)}, bf16[768,1536]{0,1:T(8,128)(2,1)}, bf16[384,768]{1,0:T(8,128)(2,1)}, bf16[1536,768]{1,0:T(8,128)(2,1)}), (bf16[768,3,384]{0,2,1:T(8,128)(2,1)}, bf16[768,1536]{0,1:T(8,128)(2,1)}, ...) | async-done | bytes 7077904 | tf_op jit(solution)/shard_map/psum | solution.py:311
  680.4 2.6 copy.41
  683.0 4.7 copy.42
  687.7 2.5 convert_element_type.31
  (112 shorter events, 49.4 us)
Async XLA Ops:
  7.2 168.7 %copy-start = (s32[2,1]{0,1:T(1,128)S(1)}, s32[2,1]{0,1:T(1,128)}, u32[]{:S(2)}) copy-start(s32[2,1]{0,1:T(1,128)} %param.17) | copy-start | bytes 28
  7.2 7.4 %copy-start.6 = (bf16[768,3,384]{2,0,1:T(8,128)(2,1)S(1)}, bf16[768,3,384]{2,0,1:T(8,128)(2,1)}, u32[]{:S(2)}) copy-start(bf16[768,3,384]{2,0,1:T(8,128)(2,1)} %param.20) | copy-start | bytes 5308420
  7.2 9.5 %copy-start.21 = (f32[2,384]{1,0:T(2,128)S(1)}, f32[2,384]{1,0:T(2,128)}, u32[]{:S(2)}) copy-start(f32[2,384]{1,0:T(2,128)} %param.21) | copy-start | bytes 9220
  7.2 160.1 %copy-start.14 = (f32[1536]{0:T(1024)S(1)}, f32[1536]{0:T(1024)}, u32[]{:S(2)}) copy-start(f32[1536]{0:T(1024)} %param.27) | copy-start | bytes 18436
  7.2 670.9 %all-reduce.3.cloned.1.call-start = ((), (), s32[]{:S(2)}) async-start(), calls=%async_computation | async-start | bytes 14155776 | tf_op jit(solution)/shard_map/psum | solution.py:311
  11.7 207.8 %collective-permute-start.5 = (bf16[768,1536]{0,1:T(8,128)(2,1)}, bf16[768,1536]{0,1:T(8,128)(2,1)}, u32[]{:S(2)}, u32[]{:S(2)}) collective-permute-start(bf16[768,1536]{0,1:T(8,128)(2,1)} %copy.33), channel_id=1, source_target_pairs={{0,1},{1,0},{2,3},{3,2},{4,5},{5,4},{6,7},{7,6},{8,9},{9,8},{10,11... | collective-permute-start | bytes 7077896 | tf_op jit(solution)/shard_map/ppermute | solution.py:277
  14.6 213.6 %collective-permute-start.7 = (bf16[1536,768]{1,0:T(8,128)(2,1)}, bf16[1536,768]{1,0:T(8,128)(2,1)}, u32[]{:S(2)}, u32[]{:S(2)}) collective-permute-start(bf16[1536,768]{1,0:T(8,128)(2,1)} %param.28), channel_id=1, source_target_pairs={{0,1},{1,0},{2,3},{3,2},{4,5},{5,4},{6,7},{7,6},{8,9},{9,8},{10,11... | collective-permute-start | bytes 7077896 | tf_op jit(solution)/shard_map/ppermute | solution.py:277
  14.6 195.3 %collective-permute-start.2 = (bf16[3,768,384]{2,1,0:T(8,128)(2,1)S(1)}, bf16[3,768,384]{2,1,0:T(8,128)(2,1)}, u32[]{:S(2)}, u32[]{:S(2)}) collective-permute-start(bf16[3,768,384]{2,1,0:T(8,128)(2,1)S(1)} %bitcast.53), channel_id=1, source_target_pairs={{0,1},{1,0},{2,3},{3,2},{4,5},{5,4},{6,7},{7,6},{8,9},{9,8},{10,11... | collective-permute-start | bytes 5308424 | tf_op jit(solution)/shard_map/ppermute | solution.py:277
  16.6 158.4 %collective-permute-start.4 = (bf16[384,768]{1,0:T(8,128)(2,1)}, bf16[384,768]{1,0:T(8,128)(2,1)}, u32[]{:S(2)}, u32[]{:S(2)}) collective-permute-start(bf16[384,768]{1,0:T(8,128)(2,1)} %param.22), channel_id=1, source_target_pairs={{0,1},{1,0},{2,3},{3,2},{4,5},{5,4},{6,7},{7,6},{8,9},{9,8},{10,11... | collective-permute-start | bytes 1769480 | tf_op jit(solution)/shard_map/ppermute | solution.py:277
  16.7 150.6 %collective-permute-start.3 = (f32[2,384]{1,0:T(2,128)S(1)}, f32[2,384]{1,0:T(2,128)S(1)}, u32[]{:S(2)}, u32[]{:S(2)}) collective-permute-start(f32[2,384]{1,0:T(2,128)S(1)} %copy-done.21), channel_id=1, source_target_pairs={{0,1},{1,0},{2,3},{3,2},{4,5},{5,4},{6,7},{7,6},{8,9},{9,8},{10,11... | collective-permute-start | bytes 9224 | tf_op jit(solution)/shard_map/ppermute | solution.py:277
  167.3 4.1 collective-permute-start.6
  171.4 7.4 %copy-start.19 = (f32[768]{0:T(1024)S(1)}, f32[768]{0:T(1024)}, u32[]{:S(2)}) copy-start(f32[768]{0:T(1024)} %param.25) | copy-start | bytes 9220
  171.4 8.0 %copy-start.20 = (f32[768]{0:T(1024)S(1)}, f32[768]{0:T(1024)}, u32[]{:S(2)}) copy-start(f32[768]{0:T(1024)} %param.29) | copy-start | bytes 9220
  171.5 20.9 %collective-permute-start = (bf16[512,768]{1,0:T(8,128)(2,1)}, bf16[512,768]{1,0:T(8,128)(2,1)}, u32[]{:S(2)}, u32[]{:S(2)}) collective-permute-start(bf16[512,768]{1,0:T(8,128)(2,1)} %get-tuple-element.65), channel_id=1, source_target_pairs={{0,1},{1,0},{2,3},{3,2},{4,5},{5,4},{6,7},{7,6},{8,9},{9,8},{10,11... | collective-permute-start | bytes 2359304 | tf_op jit(solution)/shard_map/ppermute | solution.py:277
  175.1 31.8 %collective-permute-start.1 = (bf16[512,768]{1,0:T(8,128)(2,1)}, bf16[512,768]{1,0:T(8,128)(2,1)}, u32[]{:S(2)}, u32[]{:S(2)}) collective-permute-start(bf16[512,768]{1,0:T(8,128)(2,1)} %get-tuple-element.63), channel_id=1, source_target_pairs={{0,1},{1,0},{2,3},{3,2},{4,5},{5,4},{6,7},{7,6},{8,9},{9,8},{10,11... | collective-permute-start | bytes 2359304 | tf_op jit(solution)/shard_map/ppermute | solution.py:277
  356.3 7.1 %copy-start.3 = (bf16[3072,768]{1,0:T(8,128)(2,1)S(1)}, bf16[3072,768]{1,0:T(8,128)(2,1)}, u32[]{:S(2)}) copy-start(bf16[3072,768]{1,0:T(8,128)(2,1)} %get-tuple-element.31) | copy-start | bytes 14155780
  359.7 155.7 %collective-permute-start.13 = (bf16[3,768,512]{2,1,0:T(8,128)(2,1)}, bf16[3,768,512]{2,1,0:T(8,128)(2,1)}, u32[]{:S(2)}, u32[]{:S(2)}) collective-permute-start(bf16[3,768,512]{2,1,0:T(8,128)(2,1)} %slice.77), channel_id=1, source_target_pairs={{0,1},{1,0},{2,3},{3,2},{4,5},{5,4},{6,7},{7,6},{8,9},{9,8},{10,11... | collective-permute-start | bytes 7077896 | tf_op jit(solution)/shard_map/ppermute | solution.py:277
  361.9 150.9 %collective-permute-start.10 = (bf16[3,768,384]{2,1,0:T(8,128)(2,1)S(1)}, bf16[3,768,384]{2,1,0:T(8,128)(2,1)S(1)}, u32[]{:S(2)}, u32[]{:S(2)}) collective-permute-start(bf16[3,768,384]{2,1,0:T(8,128)(2,1)S(1)} %slice.67), channel_id=1, source_target_pairs={{0,1},{1,0},{2,3},{3,2},{4,5},{5,4},{6,7},{7,6},{8,9},{9,8},{10,11... | collective-permute-start | bytes 5308424 | tf_op jit(solution)/shard_map/ppermute | solution.py:277
  363.4 149.4 %copy-start.4 = (bf16[6,768,384]{2,1,0:T(8,128)(2,1)S(1)}, bf16[6,768,384]{2,1,0:T(8,128)(2,1)}, u32[]{:S(2)}) copy-start(bf16[6,768,384]{2,1,0:T(8,128)(2,1)} %get-tuple-element.26) | copy-start | bytes 10616836
  365.0 155.4 %collective-permute-start.14 = (bf16[1536,768]{1,0:T(8,128)(2,1)}, bf16[1536,768]{1,0:T(8,128)(2,1)}, u32[]{:S(2)}, u32[]{:S(2)}) collective-permute-start(bf16[1536,768]{1,0:T(8,128)(2,1)} %slice.80), channel_id=1, source_target_pairs={{0,1},{1,0},{2,3},{3,2},{4,5},{5,4},{6,7},{7,6},{8,9},{9,8},{10,11... | collective-permute-start | bytes 7077896 | tf_op jit(solution)/shard_map/ppermute | solution.py:277
  365.6 146.3 %collective-permute-start.12 = (bf16[384,768]{1,0:T(8,128)(2,1)S(1)}, bf16[384,768]{1,0:T(8,128)(2,1)S(1)}, u32[]{:S(2)}, u32[]{:S(2)}) collective-permute-start(bf16[384,768]{1,0:T(8,128)(2,1)S(1)} %slice.72), channel_id=1, source_target_pairs={{0,1},{1,0},{2,3},{3,2},{4,5},{5,4},{6,7},{7,6},{8,9},{9,8},{10,11... | collective-permute-start | bytes 1769480 | tf_op jit(solution)/shard_map/ppermute | solution.py:277
  526.8 130.8 %collective-permute-start.8 = (bf16[512,768]{1,0:T(8,128)(2,1)}, bf16[512,768]{1,0:T(8,128)(2,1)S(1)}, u32[]{:S(2)}, u32[]{:S(2)}) collective-permute-start(bf16[512,768]{1,0:T(8,128)(2,1)} %get-tuple-element.61), channel_id=1, source_target_pairs={{0,1},{1,0},{2,3},{3,2},{4,5},{5,4},{6,7},{7,6},{8,9},{9,8},{10,11... | collective-permute-start | bytes 2359304 | tf_op jit(solution)/shard_map/ppermute | solution.py:277
  528.1 131.5 %collective-permute-start.9 = (bf16[512,768]{1,0:T(8,128)(2,1)}, bf16[512,768]{1,0:T(8,128)(2,1)S(1)}, u32[]{:S(2)}, u32[]{:S(2)}) collective-permute-start(bf16[512,768]{1,0:T(8,128)(2,1)} %get-tuple-element.59), channel_id=1, source_target_pairs={{0,1},{1,0},{2,3},{3,2},{4,5},{5,4},{6,7},{7,6},{8,9},{9,8},{10,11... | collective-permute-start | bytes 2359304 | tf_op jit(solution)/shard_map/ppermute | solution.py:277
  529.9 66.7 %collective-permute-start.11 = (f32[6,384]{1,0:T(8,128)S(1)}, f32[6,384]{1,0:T(8,128)S(1)}, u32[]{:S(2)}, u32[]{:S(2)}) collective-permute-start(f32[6,384]{1,0:T(8,128)S(1)} %fusion.5), channel_id=1, source_target_pairs={{0,1},{1,0},{2,3},{3,2},{4,5},{5,4},{6,7},{7,6},{8,9},{9,8},{10,11... | collective-permute-start | bytes 27656 | tf_op jit(solution)/shard_map/ppermute | solution.py:277
  (14 other events, 53.6 us)
Sparse Core Ops, SparseCore 0:
  524.6 153.5 all-reduce.2

commit v2 on v1

v2 whole, which is shorter than its diff:
```python
import functools

import jax
import jax.numpy as jnp
from jax import lax
from jax.experimental import pallas as pl
from jax.experimental.pallas import tpu as pltpu
from jax.sharding import PartitionSpec as P

F = jnp.float32
B = jnp.bfloat16
T = 1024
D = 768
HD = 64
HW = 384
FF = 3072
FH = 1536
CH = 512
RT = 256
QB = 256
NP = 6
EPS = 1e-05
SB = 48 ** (-0.5)
RC = 0.7978845608028654
CC = 0.044715


def nn(a, b):
    return lax.dot_general(a, b, (((1,), (0,)), ((), ())), preferred_element_type=F)


def nt(a, b):
    return lax.dot_general(a, b, (((1,), (1,)), ((), ())), preferred_element_type=F)


def tn(a, b):
    return lax.dot_general(a, b, (((0,), (0,)), ((), ())), preferred_element_type=F)


def rows_of(r):
    return pl.ds(pl.multiple_of(r * RT, RT), RT)


def norm(v):
    cen = v - jnp.mean(v, axis=-1, keepdims=True)
    inv = lax.rsqrt(jnp.mean(cen * cen, axis=-1, keepdims=True) + EPS)
    return cen * inv, inv


def norm_back(e, n, inv):
    return inv * (e - jnp.mean(e, axis=-1, keepdims=True) - n * jnp.mean(e * n, axis=-1, keepdims=True))


def gelu_pair(u):
    u2 = u * u
    t = jnp.tanh(RC * (u + CC * u2 * u))
    hp = 0.5 * (1.0 + t)
    return u * hp, hp + (0.5 * RC) * u * (1.0 - t * t) * (1.0 + (3.0 * CC) * u2)


def pair_attention(hp, n, qkv, o, lse):
    off = pl.multiple_of(hp * 128, 128)
    lane = lax.broadcasted_iota(jnp.int32, (QB, 128), 1)
    for qb in range(T // QB):
        ext = (qb + 1) * QB
        q2 = qkv[pl.ds(qb * QB, QB), pl.ds(off, 128)]
        k2 = qkv[pl.ds(0, ext), pl.ds(D + off, 128)]
        v2 = qkv[pl.ds(0, ext), pl.ds(2 * D + off, 128)]
        key = lax.broadcasted_iota(jnp.int32, (ext, QB), 0)
        qi = lax.broadcasted_iota(jnp.int32, (ext, QB), 1) + qb * QB
        bound = jnp.minimum(qi + 1, n)
        outs = []
        for h in range(2):
            qm = jnp.where((lane // HD) == h, q2, jnp.zeros_like(q2))
            s = jnp.where(key < bound, nt(k2, qm), -1e30)
            m = jnp.max(s, axis=0, keepdims=True)
            e = jnp.exp(s - m)
            l = jnp.sum(e, axis=0, keepdims=True)
            pb = (e * (1.0 / l)).astype(B)
            outs.append(tn(pb, v2))
            lse[pl.ds(hp * 2 + h, 1), pl.ds(qb * QB, QB)] = m + jnp.log(l)
        o[pl.ds(qb * QB, QB), pl.ds(off, 128)] = jnp.where(lane < HD, outs[0], outs[1]).astype(B)


def pair_backward(hp, n, qkv, do, o, lse, acc):
    off = pl.multiple_of(hp * 128, 128)
    lane = lax.broadcasted_iota(jnp.int32, (QB, 128), 1)
    for qb in reversed(range(T // QB)):
        ext = (qb + 1) * QB
        rq = pl.ds(qb * QB, QB)
        q2 = qkv[rq, pl.ds(off, 128)]
        k2 = qkv[pl.ds(0, ext), pl.ds(D + off, 128)]
        v2 = qkv[pl.ds(0, ext), pl.ds(2 * D + off, 128)]
        do2 = do[rq, pl.ds(off, 128)]
        o2 = o[rq, pl.ds(off, 128)]
        prod = (do2.astype(F) * o2.astype(F)).T
        key = lax.broadcasted_iota(jnp.int32, (ext, QB), 0)
        qi = lax.broadcasted_iota(jnp.int32, (ext, QB), 1) + qb * QB
        bound = jnp.minimum(qi + 1, n)
        dqs, dks, dvs = [], [], []
        for h in range(2):
            hm = (lane // HD) == h
            qm = jnp.where(hm, q2, jnp.zeros_like(q2))
            dm = jnp.where(hm, do2, jnp.zeros_like(do2))
            dd = jnp.sum(prod[h * HD : (h + 1) * HD], axis=0, keepdims=True)
            ls = lse[pl.ds(hp * 2 + h, 1), rq]
            p = jnp.where(key < bound, jnp.exp(nt(k2, qm) - ls), 0.0)
            ds = (p * (nt(v2, dm) - dd)).astype(B)
            dqs.append(tn(k2, ds).T)
            dks.append(nn(ds, qm))
            dvs.append(nn(p.astype(B), dm))
        qkv[rq, pl.ds(off, 128)] = (jnp.where(lane < HD, dqs[0], dqs[1]) * 0.125).astype(B)
        dk = dks[0] + dks[1]
        dv = dvs[0] + dvs[1]
        if qb == T // QB - 1:
            acc[:, 0:128] = dk
            acc[:, 128:256] = dv
        else:
            acc[pl.ds(0, ext), 0:128] += dk
            acc[pl.ds(0, ext), 128:256] += dv
    qkv[:, pl.ds(D + off, 128)] = acc[:, 0:128].astype(B)
    qkv[:, pl.ds(2 * D + off, 128)] = acc[:, 128:256].astype(B)


def phase_mid(n, x, c, o, wproj, bproj, g2, s2, r1, a2, dm, put):
    def row(r, ob):
        rr = rows_of(r)
        v = x[rr, :].astype(F) + SB * (nn(o[rr, :], wproj[...]) + bproj[...])
        r1[rr, :] = v
        n2, _inv = norm(v)
        a2[rr, :] = (n2 * g2[...] + s2[...]).astype(B)
        ids = lax.broadcasted_iota(jnp.int32, (RT, 1), 0) + r * RT
        cs = SB * (c[rr, :].astype(F) * (ids < n).astype(F))
        dm[rr, :] = cs.astype(B)
        return ob + jnp.sum(cs, axis=0, keepdims=True)

    put(5, lax.fori_loop(0, T // RT, row, jnp.zeros((1, D), F)))


def phase_back(n, c, r1, m, da2, bout, g2, wproj, dattn, do, out, put):
    def row(r, acc):
        rr = rows_of(r)
        v = r1[rr, :]
        out[rr, :] = (v + SB * (m[rr, :] + bout[...])).astype(B)
        n2, inv = norm(v)
        g = da2[rr, :]
        ids = lax.broadcasted_iota(jnp.int32, (RT, 1), 0) + r * RT
        dr = c[rr, :].astype(F) * (ids < n).astype(F) + norm_back(g * g2[...], n2, inv)
        da2[rr, :] = dr
        sr = SB * dr
        sb = sr.astype(B)
        dattn[rr, :] = sb
        do[rr, 0:D] = nt(sb, wproj[...]).astype(B)
        total = lambda w: jnp.sum(w, axis=0, keepdims=True)
        return acc[0] + total(g * n2), acc[1] + total(g), acc[2] + total(sr)

    z = jnp.zeros((1, D), F)
    a, b, p = lax.fori_loop(0, T // RT, row, (z, z, z))
    put(2, p)
    put(3, a)
    put(4, b)


def phase_end(x, qkv, wqkv, g1, dr1, gin, put):
    def row(r, acc):
        rr = rows_of(r)
        g = nt(qkv[rr, :], wqkv[...])
        n1, inv = norm(x[rr, :].astype(F))
        gin[rr, :] = (dr1[rr, :] + norm_back(g * g1[...], n1, inv)).astype(B)
        total = lambda w: jnp.sum(w, axis=0, keepdims=True)
        return acc[0] + total(g * n1), acc[1] + total(g)

    z = jnp.zeros((1, D), F)
    a, b = lax.fori_loop(0, T // RT, row, (z, z))
    put(0, a)
    put(1, b)


MESH = pl.DeviceIdType.MESH
NJ = 3
WA = 256
WB = 128
MLP0 = 0
BACK = 6
BWD0 = 7
END = 13


def each(n, fn):
    if n <= 3:
        for d in range(1, n + 1):
            fn(d)
    else:
        lax.fori_loop(1, n + 1, lambda d, _: (fn(d), 0)[1], 0)


def add_rows(rows, dst, srcs):
    step = next(s for s in (192, 128, 64, 32, 16) if rows % s == 0)

    def tile(i, _):
        rr = pl.ds(pl.multiple_of(i * step, step), step)
        v = dst[rr, :].astype(F)
        for s in srcs:
            v = v + s[rr, :].astype(F)
        dst[rr, :] = v.astype(dst.dtype)
        return 0

    lax.fori_loop(0, rows // step, tile, 0)


def depth(dp):
    return (dp // 16 - 1).bit_length()


def mlp_chunk(w1, w2, bias, a2, dm, m, da2, hd, piece):
    tot = jnp.zeros((1, CH), F)
    for r in range(T // RT):
        rr = pl.ds(r * RT, RT)
        u = nn(a2[rr, :], w1[...]) + bias
        h, sl = gelu_pair(u)
        hb = h.astype(B)
        hd[rr, 0:CH] = hb
        du = (nt(dm[rr, :], w2[...]) * sl).astype(B)
        hd[rr, CH : 2 * CH] = du
        m[rr, :] += nn(hb, w2[...])
        da2[rr, :] += nt(du, w1[...])
        tot = tot + jnp.sum(du.astype(F), axis=0, keepdims=True)
    for k in range(D // 256):
        g = tn(a2[:, k * 256 : (k + 1) * 256], hd[:, CH : 2 * CH]).astype(B)
        for b in range(CH // WA):
            piece[b * D + k * 256 : b * D + (k + 1) * 256, :] = g[:, b * WA : (b + 1) * WA]
    base = CH // WA * D
    for k in range(CH // 256):
        g = tn(hd[:, k * 256 : (k + 1) * 256], dm[...]).astype(B)
        for b in range(D // WA):
            piece[base + b * CH + k * 256 : base + b * CH + (k + 1) * 256, :] = g[:, b * WA : (b + 1) * WA]
    return tot


def kernel(dp, lens, inp, cot, g1, s1, wq, bq, wp, bproj, g2, s2, wf, bf, wo, bout,
           out, gin, gq, gp, gf, go, sm, lf, lo,
           xf, cf, a1t, wqkv, wproj, bqo, bfo, wb1, wb2, qkv, o, lse, r1, a2, dm, m, da2, hd,
           pa, ca, xa, ya, za, ga, pb, xb, yb, zb, ps, cs, xs, ys, zs, gs, ss, rs, ls, ready):
    ti = lax.axis_index("tensor")
    me = lax.axis_index("dp")
    nz = 4
    cc = lax.rem(me, 2)
    yy = lax.rem(me // 2, 2)
    zi = lax.rem(me // 4, nz)
    beyond = [{"dp": me + (1 - 2 * lax.rem(me // (16 << b), 2)) * (16 << b)} for b in range(depth(dp))]
    z1 = lax.rem(zi, 2)
    X = {"tensor": 1 - ti}
    C = {"dp": me + 1 - 2 * cc}
    Y = {"dp": me + 2 - 4 * yy}
    Z1 = {"dp": me + 4 - 8 * z1}
    zp = lambda k: {"dp": me + (k - zi) * 4}
    al = pl.multiple_of
    count = [0]
    flags = [0]

    def new(k=1):
        count[0] += k
        return count[0] - k

    def rc(src, dst, i, dev, j=None):
        return pltpu.make_async_remote_copy(src_ref=src, dst_ref=dst, send_sem=ss.at[i], recv_sem=rs.at[i if j is None else j],
                                            device_id=dev, device_id_type=MESH)

    bar = pltpu.get_barrier_semaphore()
    for dev in (X, C, Y):
        pl.semaphore_signal(bar, inc=1, device_id=dev, device_id_type=MESH)
    each(nz - 1, lambda d: pl.semaphore_signal(bar, inc=1, device_id=zp(lax.rem(zi + d, nz)), device_id_type=MESH))
    for dev in beyond:
        pl.semaphore_signal(bar, inc=1, device_id=dev, device_id_type=MESH)
    pl.semaphore_wait(bar, 3 + nz - 1 + len(beyond))

    def units(group):
        if group == 0:
            return [(wq.at[t], lambda r, t=t: wqkv.at[r, t * D + HW : (t + 1) * D], D) for t in range(3)]
        j = group - 1
        cols = slice(j * CH, (j + 1) * CH)
        res = [(wf.at[:, cols], lambda r: lf.at[r, cols], D),
               (wo.at[cols, :], lambda r: lo.at[pl.ds(al(j * CH + r.start, 16), r.size), :], CH)]
        if group == 1:
            res.append((wp, lambda r: wproj.at[pl.ds(al(HW + r.start, 16), r.size), :], HW))
        return res

    wsem = [new(4 * len(units(g))) for g in range(4)]

    def wcopies(group, stage):
        res = []
        for i, (own, land, n) in enumerate(units(group)):
            e = n // 8
            if stage < 2:
                r = pl.ds(al((cc * 4 + yy * 2 + z1) * e, 16), e)
            elif stage == 2:
                r = pl.ds(al((cc * 2 + yy) * 2 * e, 16), 2 * e)
            else:
                r = pl.ds(al(cc * 4 * e, 16), 4 * e)
            src = own.at[r, :] if stage == 0 else land(r)
            res.append(rc(src, land(r), wsem[group] + stage * len(units(group)) + i, (X, Z1, Y, C)[stage]))
        return res

    def wsend(group, stage):
        for c in wcopies(group, stage):
            c.start()

    def wstep(group, stage):
        for c in wcopies(group, stage):
            c.wait()
        if stage < 3:
            wsend(group, stage + 1)

    half = lambda i: pl.ds(al(i * (T // 2), T // 2), T // 2)
    si = new(8)
    x_copy = rc(inp.at[1 - ti], xf.at[half(ti)], si, X)
    c_copy = rc(cot.at[1 - ti], cf.at[half(ti)], si + 1, X)
    bq_copy = rc(bq, bqo, si + 2, X)
    bf_copy = rc(bf, bfo, si + 3, X)
    out_copy = rc(a2.at[half(1 - ti)], out.at[ti], si + 4, X)
    gin_copy = rc(dm.at[half(1 - ti)], gin.at[ti], si + 5, X)
    local = [pltpu.make_async_copy(inp.at[ti], xf.at[half(ti)], ls.at[0]),
             pltpu.make_async_copy(cot.at[ti], cf.at[half(ti)], ls.at[1]),
             pltpu.make_async_copy(wp, wproj.at[0:HW], ls.at[2])]
    local += [pltpu.make_async_copy(wq.at[t], wqkv.at[:, t * D : t * D + HW], ls.at[3 + t]) for t in range(3)]
    wsend(0, 0)
    bq_copy.start()
    x_copy.start()
    for c in local:
        c.start()
    bf_copy.start()
    wsend(1, 0)
    wsend(2, 0)
    c_copy.start()
    wsend(3, 0)

    n = lens[ti, 0]

    def make_set(k_pieces, rows, buf, co, xr, yr, zr, gr, x_first):
        h, q = rows // 2, rows // 4
        s = q // nz
        base = [new(9 + 4 * nz + len(beyond)) for _ in range(k_pieces)]
        flag = flags[0]
        flags[0] += 3 * k_pieces
        mine = al(cc * h, 16)
        keep = al(cc * h + yy * q, 16)
        give = al(cc * h + (1 - yy) * q, 16)
        shard = lambda k: pl.ds(al(keep + k * s, 8), s)

        def swap_c(j):
            r = pl.ds(al((1 - cc) * h, 16), h)
            return [rc(buf(w, j, r), co(j, w), base[j] + w, C) for w in (0, 1)]

        def swap_x(j):
            src = buf(1, j, pl.ds(mine, h)) if x_first else buf(1, j, pl.ds(keep, q))
            return [rc(src, xr.at[j], base[j] + 2, X)]

        def swap_y(j):
            return [rc(buf(w, j, pl.ds(give, q)), yr.at[j, w], base[j] + 3 + w, Y) for w in range(yr.shape[1])]

        def z_out(j):
            each(nz - 1, lambda d: z_one(j, d).start())

        def z_one(j, d):
            k = lax.rem(zi + d, nz)
            return rc(buf(0, j, shard(k)), zr.at[j, zi], base[j] + 9 + k, zp(k), base[j] + 9 + nz + zi)

        def z_in(j):
            def one(d):
                z_one(j, d).wait_send()
                k = lax.rem(zi + d, nz)
                rc(zr.at[j, k], zr.at[j, k], base[j] + 9 + k, zp(k), base[j] + 9 + nz + k).wait_recv()

            each(nz - 1, one)

        def za_one(j, d):
            k = lax.rem(zi + d, nz)
            return rc(buf(0, j, shard(zi)), buf(0, j, shard(zi)), base[j] + 9 + 2 * nz + k, zp(k), base[j] + 9 + 3 * nz + zi)

        def za_in(j):
            def one(d):
                za_one(j, d).wait_send()
                k = lax.rem(zi + d, nz)
                rc(buf(0, j, shard(k)), buf(0, j, shard(k)), base[j] + 9 + 2 * nz + k, zp(k), base[j] + 9 + 3 * nz + k).wait_recv()

            each(nz - 1, one)

        def all_y(j):
            r = pl.ds(keep, q)
            return rc(buf(0, j, r), buf(0, j, r), base[j] + 5, Y)

        def all_c(j):
            r = pl.ds(mine, h)
            return rc(buf(0, j, r), buf(0, j, r), base[j] + 6, C)

        def start(cs):
            for c in cs:
                c.start()

        def wait(cs):
            for c in cs:
                c.wait()

        def free(j, i, dev):
            pl.semaphore_signal(ready.at[flag + 3 * j + i], inc=1, device_id=dev, device_id_type=MESH)

        def freed(j, i, k):
            pl.semaphore_wait(ready.at[flag + 3 * j + i], k)

        def s0(j):
            start(swap_c(j))

        def s1_(j):
            wait(swap_c(j))
            free(j, 0, C)
            for w in (1, 0):
                add_rows(h, buf(w, j, pl.ds(mine, h)), [co(j, w)])
                if w == 1 and x_first:
                    start(swap_x(j))
            if not x_first:
                start(swap_y(j))

        def s2_(j):
            if x_first:
                wait(swap_x(j))
                add_rows(h, buf(0, j, pl.ds(mine, h)), [xr.at[j]])
                start(swap_y(j))
            else:
                wait(swap_y(j))
                free(j, 1, Y)
                for w in (1, 0):
                    add_rows(q, buf(w, j, pl.ds(keep, q)), [yr.at[j, w]])
                    if w == 1:
                        start(swap_x(j))

        def s3_(j):
            if x_first:
                wait(swap_y(j))
                free(j, 1, Y)
                add_rows(q, buf(0, j, pl.ds(keep, q)), [yr.at[j, 0]])
            else:
                wait(swap_x(j))
                add_rows(q, buf(0, j, pl.ds(keep, q)), [xr.at[j]])
            z_out(j)

        def s4_(j):
            z_in(j)
            each(nz - 1, lambda d: free(j, 2, zp(lax.rem(zi + d, nz))))
            add_rows(s, buf(0, j, shard(zi)), [zr.at[j, lax.rem(zi + d, nz)] for d in range(1, nz)])
            for b, dev in enumerate(beyond):
                copy = rc(buf(0, j, shard(zi)), gr(j, b), base[j] + 9 + 4 * nz + b, dev)
                copy.start()
                copy.wait()
                add_rows(s, buf(0, j, shard(zi)), [gr(j, b)])
            freed(j, 2, nz - 1)
            each(nz - 1, lambda d: za_one(j, d).start())

        def s5_(j):
            za_in(j)
            freed(j, 1, 1)
            all_y(j).start()

        def s6_(j):
            all_y(j).wait()
            freed(j, 0, 1)
            all_c(j).start()

        def s7_(j):
            all_c(j).wait()

        return [s0, s1_, s2_, s3_, s4_, s5_, s6_, s7_]

    ra = pa.shape[2]
    lanes = slice(0, WB)
    set_a = make_set(NJ, ra, lambda w, j, r: pa.at[w, j, r], lambda j, w: ca.at[j, w], xa, ya, za, lambda j, b: ga.at[j % 2, b], True)
    buf_b = lambda w, j, r: pa.at[1, j, r, lanes] if w else pb.at[j, r]
    set_b = make_set(NJ, ra, buf_b, lambda j, w: ca.at[j, w, :, lanes], xb, yb, zb, lambda j, b: ga.at[(j + 1) % 2, b, :, lanes], False)
    set_s = make_set(1, ps.shape[2], lambda w, j, r: ps.at[w, j, r], lambda j, w: cs.at[j, w], xs, ys, zs, lambda j, b: gs.at[0, b], False)

    def out_a(j):
        own = pa.at[0, j]
        res = [(own.at[b * D : (b + 1) * D], gf.at[:, j * CH + b * WA : j * CH + (b + 1) * WA]) for b in range(CH // WA)]
        base = CH // WA * D
        res += [(own.at[base + b * CH : base + (b + 1) * CH], go.at[j * CH : (j + 1) * CH, b * WA : (b + 1) * WA])
                for b in range(D // WA)]
        return [pltpu.make_async_copy(u, v, ls.at[8 + j * 5 + i]) for i, (u, v) in enumerate(res)]

    def out_b(j):
        own = pb.at[j]
        res = [(own.at[t * D : (t + 1) * D], gq.at[t, :, j * WB : (j + 1) * WB]) for t in range(3)]
        res += [(own.at[3 * D + b * WB : 3 * D + (b + 1) * WB], gp.at[j * WB : (j + 1) * WB, b * WB : (b + 1) * WB])
                for b in range(D // WB)]
        return [pltpu.make_async_copy(u, v, ls.at[23 + j * 9 + i]) for i, (u, v) in enumerate(res)]

    def a_step(j, s):
        def run():
            set_a[s](j)
            if s == 7:
                for c in out_a(j):
                    c.start()
        return run

    def b_step(j, s):
        def run():
            set_b[s](j)
            if s == 7:
                for c in out_b(j):
                    c.start()
        return run

    events = {}

    def at(tick, fn):
        events.setdefault(tick, []).append(fn)

    a_ticks = [[1, 2, 6, 8, 10, 12], [3, 4, 8, 10, 12, 13], [5, 6, 11, 13]]
    b_ticks = [[8, 9, 11, 13], [10, 11, 13], [12, 13]]
    pos_a, pos_b = [], []
    for j in range(NJ):
        for s, tick in enumerate(a_ticks[j]):
            at(tick, a_step(j, s))
        for s, tick in enumerate(b_ticks[j]):
            at(tick, b_step(j, s))
        pos_a.append(len(a_ticks[j]))
        pos_b.append(len(b_ticks[j]))

    def ticks(first, last, t):
        for g in range(first, last):
            if g in events:
                @pl.when(t + first == g)
                def _(g=g):
                    for fn in events[g]:
                        fn()

    def put(i, v):
        for w in (0, 1):
            for b in range(D // 128):
                ps[w, 0, i * 8 + b : i * 8 + b + 1, :] = v[:, b * 128 : (b + 1) * 128]

    ps[...] = jnp.zeros_like(ps)

    wstep(0, 0)
    wstep(0, 1)
    local[0].wait()
    x_copy.wait()

    def ln_row(r, _):
        rr = rows_of(r)
        n1, _inv = norm(xf[rr, :].astype(F))
        a = (n1 * g1[...] + s1[...]).astype(B)
        a2[rr, :] = a
        a1t[:, rr] = a.T
        return 0

    lax.fori_loop(0, T // RT, ln_row, 0)
    wstep(0, 2)
    bq_copy.wait()
    for c in local[3:]:
        c.wait()
    wstep(0, 3)
    wstep(1, 0)

    def qkv_row(r, _):
        rr = rows_of(r)
        a = a2[rr, :]
        for t in range(3):
            v = nn(a, wqkv[:, t * D : (t + 1) * D])
            for k, b in enumerate((bq, bqo)):
                u = v[:, k * HW : (k + 1) * HW]
                if t != 1:
                    u = u + b[t // 2 : t // 2 + 1, :]
                if t == 0:
                    u = u * 0.125
                qkv[rr, t * D + k * HW : t * D + (k + 1) * HW] = u.astype(B)
        return 0

    lax.fori_loop(0, T // RT, qkv_row, 0)

    def fwd(hp, _):
        pair_attention(hp, n, qkv, o, lse)
        for t, fns in ((1, [(1, 1), (2, 0)]), (3, [(2, 1)]), (4, [(1, 2)])):
            @pl.when(hp == t)
            def _(fns=fns):
                for f in fns:
                    wstep(*f)
        return 0

    lax.fori_loop(0, NP, fwd, 0)
    local[1].wait()
    local[2].wait()
    wstep(1, 3)
    c_copy.wait()
    bf_copy.wait()

    def fetch(which, j):
        cols = pl.ds(al(j * CH, CH), CH)
        s1 = (wf if which == 0 else lf).at[:, cols]
        s2 = (wo if which == 0 else lo).at[cols, :]
        return [pltpu.make_async_copy(s1, wb1.at[which], ls.at[50 + which]),
                pltpu.make_async_copy(s2, wb2.at[which], ls.at[52 + which])]

    for c in fetch(0, 0):
        c.start()
    phase_mid(n, xf, cf, o, wproj, bproj, g2, s2, r1, a2, dm, put)
    m[...] = jnp.zeros_like(m)
    da2[...] = jnp.zeros_like(da2)

    def chunk(t, _):
        which = lax.rem(t, 2)
        j = t // 2
        for g, fns in ((0, [(2, 2), (3, 0)]), (1, [(2, 3), (3, 1)]), (3, [(3, 2)]), (4, [(3, 3)])):
            @pl.when(t == g)
            def _(fns=fns):
                for f in fns:
                    wstep(*f)
        for w in (0, 1):
            @pl.when(which == w)
            def _(w=w):
                for c in fetch(w, j):
                    c.wait()

            @pl.when((which == 1 - w) & (t < 5))
            def _(w=w):
                for c in fetch(w, (t + 1) // 2):
                    c.start()
        bias = jnp.where(which == 0, bf[j], bfo[j])
        tot = mlp_chunk(wb1.at[which], wb2.at[which], bias, a2, dm, m, da2, hd, pa.at[which, j])
        for b in range(CH // 128):
            ps[which, 0, pl.ds(64 + j * 4 + b, 1), :] = tot[:, b * 128 : (b + 1) * 128]
        ticks(0, 6, t)
        return 0

    lax.fori_loop(0, 6, chunk, 0)

    phase_back(n, cf, r1, m, da2, bout, g2, wproj, dm, hd, a2, put)
    for fn in events[6]:
        fn()
    out_copy.start()
    out_own = pltpu.make_async_copy(a2.at[half(ti)], out.at[ti], ls.at[6])
    gin_own = pltpu.make_async_copy(dm.at[half(ti)], gin.at[ti], ls.at[7])
    out_own.start()

    def bwd(t, _):
        which = lax.rem(t, 2)
        j = t // 2
        hp = which * NJ + j
        pair_backward(hp, n, qkv, hd, o, lse, m)
        off = al(hp * 128, 128)
        d = jnp.concatenate([qkv[:, pl.ds(k * D + off, 128)] for k in range(3)], axis=1)
        g = nn(a1t[...], d).astype(B)
        e = tn(o[:, pl.ds(off, 128)], dm[...]).astype(B)

        def store(piece):
            for k in range(3):
                piece[k * D : (k + 1) * D, :] = g[:, k * 128 : (k + 1) * 128]
            for b in range(D // WB):
                piece[3 * D + b * WB : 3 * D + (b + 1) * WB, :] = e[:, b * WB : (b + 1) * WB]

        @pl.when(which == 0)
        def _():
            store(pb.at[j])

        @pl.when(which == 1)
        def _():
            store(pa.at[1, j, :, lanes])

        for k, base in ((0, 48), (2, 56)):
            v = jnp.sum(qkv[:, pl.ds(k * D + off, 128)].astype(F), axis=0, keepdims=True)
            ps[which, 0, pl.ds(base + j, 1), :] = v
        ticks(7, 13, t)
        return 0

    lax.fori_loop(0, 6, bwd, 0)
    phase_end(xf, qkv, wqkv, g1, da2, dm, put)
    set_s[0](0)
    gin_copy.start()
    gin_own.start()
    for fn in events[13]:
        fn()
    pos_s = 1
    for rnd in range(8):
        for j in range(NJ):
            if pos_a[j] < 8:
                a_step(j, pos_a[j])()
                pos_a[j] += 1
        for j in range(NJ):
            if pos_b[j] < 8:
                b_step(j, pos_b[j])()
                pos_b[j] += 1
        if pos_s < 8:
            set_s[pos_s](0)
            pos_s += 1
    sm_own = pltpu.make_async_copy(ps.at[0, 0], sm, ls.at[54])
    sm_own.start()
    for j in range(NJ):
        for c in out_a(j) + out_b(j):
            c.wait()
    for c in (sm_own, out_own, gin_own, out_copy, gin_copy):
        c.wait()
    assert count[0] <= SEMS(dp)


def SEMS(dp):
    return 48 + 7 * (25 + depth(dp))


def local_call(dp, *args):
    V = pl.BlockSpec(memory_space=pltpu.VMEM)
    S = pl.BlockSpec(memory_space=pltpu.SMEM)
    A = pl.BlockSpec(memory_space=pl.ANY)
    sd = jax.ShapeDtypeStruct
    ra, rsm, nz = 4 * D, 256, 4
    nb = max(depth(dp), 1)
    outs = (sd((2, T // 2, D), B), sd((2, T // 2, D), B), sd((3, D, HW), B), sd((HW, D), B), sd((D, FH), B),
            sd((FH, D), B), sd((rsm, 128), F), sd((D, FH), B), sd((FH, D), B))
    vm = pltpu.VMEM
    sem = pltpu.SemaphoreType.DMA

    def buffers(k, r, w, x_first, dt):
        return [vm((2, k, r, w), dt), vm((k, 2, r // 2, w), dt), vm((k, r // 2 if x_first else r // 4, w), dt),
                vm((k, 1 if x_first else 2, r // 4, w), dt), vm((k, nz, r // 4 // nz, w), dt), vm((min(k, 2), nb, r // 4 // nz, w) if dp > 16 else (1, 1, 16, 128), dt)]

    return pl.pallas_call(
        functools.partial(kernel, dp),
        out_shape=outs,
        in_specs=[S, A, A, V, V, A, V, A, V, V, V, A, V, A, V],
        out_specs=(A,) * 9,
        scratch_shapes=[
            vm((T, D), B), vm((T, D), B), vm((D, T), B), vm((D, 3 * D), B), vm((D, D), B), vm((2, HW), F), vm((3, 1, CH), F),
            vm((2, D, CH), B), vm((2, CH, D), B), vm((T, 3 * D), B), vm((T, D), B), vm((16, T), F), vm((T, D), F),
            vm((T, D), B), vm((T, D), B), vm((T, D), F), vm((T, D), F), vm((T, 2 * CH), B),
        ] + buffers(NJ, ra, WA, True, B) + [vm((NJ, ra, WB), B)] + buffers(NJ, ra, WB, False, B)[2:5] + buffers(1, rsm, 128, False, F)
        + [sem((SEMS(dp),)), sem((SEMS(dp),)), sem((56,)), pltpu.SemaphoreType.REGULAR((21,))],
        compiler_params=pltpu.CompilerParams(vmem_limit_bytes=VLIMIT, collective_id=0, has_side_effects=True),
    )(*args)


VLIMIT = 63 * 2**20 + 2**19


def body(dp, inputs, cotangent, lengths, gain_one, shift_one, qkv_weight, qv_bias, proj_weight, proj_bias, gain_two,
         shift_two, fc_weight, fc_bias, out_weight, out_bias):
    row = lambda v: v.reshape(1, D)
    out, gin, gq, gp, gf, go, sm, _lf, _lo = local_call(
        dp, lengths, inputs.reshape(2, T // 2, D), cotangent.reshape(2, T // 2, D), row(gain_one), row(shift_one),
        jnp.transpose(qkv_weight, (1, 0, 2)), qv_bias, proj_weight, row(proj_bias), row(gain_two), row(shift_two),
        fc_weight, fc_bias.reshape(3, 1, CH), out_weight, row(out_bias))
    vec = lambda i: sm[i * 8 : i * 8 + 6].reshape(D)
    gqv = jnp.stack([sm[48:51].reshape(HW), sm[56:59].reshape(HW)])
    rows = lambda v: v.astype(F)[:, None]
    return (rows(out), rows(gin), vec(0), vec(1), jnp.transpose(gq.astype(F), (1, 0, 2)), gqv, gp.astype(F), vec(2), vec(3),
            vec(4), gf.astype(F), sm[64:76].reshape(FH), go.astype(F), vec(5))


def solution(mesh):
    dp = P(None, "dp", "tensor", None)
    return jax.shard_map(
        functools.partial(body, mesh.shape["dp"]),
        mesh=mesh,
        in_specs=(dp, dp, P(None, "dp"), P(), P(), P(None, None, "tensor"), P(None, "tensor"), P("tensor", None), P(),
                  P(), P(), P(None, "tensor"), P("tensor"), P("tensor", None), P()),
        out_specs=(dp, dp, P(), P(), P(None, None, "tensor"), P(None, "tensor"), P("tensor", None), P(), P(), P(),
                   P(None, "tensor"), P("tensor"), P("tensor", None), P()),
        check_vma=False,
    )
```

time: 698 us -> 259 us (0.37)
  waiting for transfers between devices: 326 us -> 0 us
  blocking collectives: 125 us -> 0 us
  Pallas kernels: 123 us -> 230 us
  local copies, waits for them, and re-layouts: 54 us -> 13.5 us
  other arithmetic: 36.7 us -> 14.3 us
  starting transfers between devices: 17.4 us -> 0 us
  between operations: 14.3 us -> 0.67 us
    ppermute x15 -> x0, waiting for transfers between devices: 309 us -> none  [body(): swap = lambda v: lax.ppermute(v, 'tensor', [(0, 1), (1, 0)])]
    psum x2 -> x0, blocking collectives: 125 us -> none  [the longest x1 65.7 us: body(): small = lax.psum(small, ('dp', 'tensor'))]
    pallas_call x1, Pallas kernels: 123 us -> 230 us  [local_call(): pl.pallas_call(functools.partial(kernel, dp), out_shape=outs, in_specs=[S...]
    ppermute x15 -> x0, starting transfers between devices: 17.4 us -> none  [body(): swap = lambda v: lax.ppermute(v, 'tensor', [(0, 1), (1, 0)])]
    psum x1 -> x0, waiting for transfers between devices: 16.6 us -> none  [total(): return lax.psum(v[:k] + swap(v[k:]), 'dp').astype(F)]
    concatenate x5 -> x0, other arithmetic: 12.1 us -> none  [the longest x1 4.87 us: body(): wout = jnp.concatenate([out_weight, swap(out_weight)])]
    unnamed x47 -> x10, local copies, waits for them, and re-layouts: 13.2 us -> 2 us
    reshape x6 -> x3, local copies, waits for them, and re-layouts: 13.9 us -> 3.94 us  [the longest x1 1.34 us: body(): vec = lambda i: sm[i * 8:i * 8 + 6].reshape(D)]
  transfers between devices with their start and end apart: 16 -> 0, of which waited for: 5 -> 0; matrix products, arithmetic and copies ran while one was open for 9% -> 0% of each run, Pallas kernels for 0% -> 0%
where the time goes in v2:
time: 259 us; the launch traced here: 258 us
  Pallas kernels  230 us (89%)
  other arithmetic  14.3 us (6%)
  local copies, waits for them, and re-layouts  13.5 us (5%)
    pallas_call x1, Pallas kernels, local_call(): pl.pallas_call(functools.partial(kernel, dp), out_shape=outs, in_specs=[S...  230 us
    reshape x6, local copies, waits for them, and re-layouts, body(): row = lambda v: v.reshape(1, D)  7.6 us
    unnamed x1, other arithmetic  5.27 us

profile of v2, /device:TPU:0, one launch (start us, length us, event | category | flops | bytes accessed | tf_op | source)
XLA Modules:
  0.0 258.1 jit_solution(5991630375863660831)
XLA Ops:
  0.6 1.3 reshape.83.bf
  1.9 1.3 reshape.78.g1
  3.2 1.3 reshape.79.s1
  4.5 1.3 reshape.80.bproj
  5.7 1.3 reshape.81.g2
  7.0 1.3 reshape.82.s2
  8.3 1.3 reshape.84.bout
  9.5 1.3 copy.29.lens
  10.8 229.6 %shard_map.254 = (bf16[2,512,768]{2,1,0:T(8,128)(2,1)}, bf16[2,512,768]{2,1,0:T(8,128)(2,1)}, bf16[3,768,384]{2,1,0:T(8,128)(2,1)}, bf16[384,768]{1,0:T(8,128)(2...) custom-call(s32[2,1]{1,0:T(2,128)} %copy.29.lens, ...), custom_call_target="tpu_custom_call" | custom-call | tf_op jit(solution)/shard_map/pallas_call | solution.py:723
  240.4 0.7 slice_bitcast_fusion.8
  241.1 0.6 pad_maximum_fusion
  241.7 0.0 copy-start.1
  241.7 5.3 %bitcast_convert_fusion = (f32[2,1,512,768]{3,2,1,0:T(8,128)}, f32[2,1,512,768]{3,2,1,0:T(8,128)}) fusion(bf16[2,512,768]{2,1,0:T(8,128)(2,1)} %get-tuple-element.22, bf16[2,512,768]{2,1,0:T(8,128)(2,1)} %get-tuple-element.21), kind=kLoop, calls=%fused_computation.1 | loop fusion | flops 1572864 | bytes 9437184
  247.0 1.3 slice_bitcast_fusion.1
  248.3 1.3 slice_bitcast_fusion
  249.6 0.0 copy-done.1
  249.6 0.0 copy-start
  249.6 2.8 %convert_element_type.13 = f32[768,1536]{1,0:T(8,128)} convert(bf16[768,1536]{1,0:T(8,128)(2,1)S(1)} %copy-done.1) | non-fusion elementwise | flops 1179648 | bytes 7077888 | tf_op jit(solution)/shard_map/convert_element_type | solution.py:752
  252.5 0.0 copy-done
  252.5 2.5 convert_element_type.14
  255.0 0.0 copy-done.2
  255.0 2.0 convert_bitcast_fusion
  257.0 0.0 copy-done.3
  257.0 1.1 convert_element_type.12
  (3 shorter events, 0.0 us)
Async XLA Ops:
  241.7 7.9 %copy-start.1 = (bf16[768,1536]{1,0:T(8,128)(2,1)S(1)}, bf16[768,1536]{1,0:T(8,128)(2,1)}, u32[]{:S(2)}) copy-start(bf16[768,1536]{1,0:T(8,128)(2,1)} %get-tuple-element.26) | copy-start | bytes 7077892
  249.6 2.8 %copy-start = (bf16[1536,768]{1,0:T(8,128)(2,1)S(1)}, bf16[1536,768]{1,0:T(8,128)(2,1)}, u32[]{:S(2)}) copy-start(bf16[1536,768]{1,0:T(8,128)(2,1)} %get-tuple-element.27) | copy-start | bytes 7077892
  252.5 2.5 copy-start.2
  255.0 2.0 copy-start.3

commit v3 on v2

--- a/solution.py
+++ b/solution.py
@@ -161,7 +161,7 @@
     put(4, b)
 
 
-def phase_end(x, qkv, wqkv, g1, dr1, gin, put):
+def phase_end(x, qkv, wqkv, g1, dr1, gin, first, sums):
     def row(r, acc):
         rr = rows_of(r)
         g = nt(qkv[rr, :], wqkv[...])
@@ -171,19 +171,67 @@
         return acc[0] + total(g * n1), acc[1] + total(g)
 
     z = jnp.zeros((1, D), F)
-    a, b = lax.fori_loop(0, T // RT, row, (z, z))
-    put(0, a)
-    put(1, b)
-
-
+    return lax.fori_loop(first, first + T // RT // 2, row, (z, z) if sums is None else sums)
+
+
+EVENTS = {
+    "ln": (),
+    "q0": ("W4.w0",),
+    "q1": (),
+    "q2": (),
+    "q3": (),
+    "f0": ("W1.w0", "W4.w1",),
+    "f1": ("W2.w0",),
+    "f2": ("W1.w1", "W4.w2",),
+    "f3": ("W2.w1", "W4.w3",),
+    "f4": (),
+    "f5": ("W1.w2",),
+    "mid0": (),
+    "mid1": ("W3.w0", "W2.w2",),
+    "mid2": ("W1.w3",),
+    "m0a": (),
+    "m0b": ("A0.cs1", "W3.w1", "W2.w3",),
+    "m1a": ("A0.cd1",),
+    "m1b": ("A0.cs0",),
+    "m2a": ("W3.w2", "A0.cd0",),
+    "m2b": ("A1.cs1",),
+    "m3a": ("W3.w3", "A0.yd1",),
+    "m3b": ("A1.cs0", "A1.cd1",),
+    "m4a": ("A0.yd0",),
+    "m4b": ("A2.cs1", "A1.cd0",),
+    "m5a": ("A0.xd",),
+    "m5b": ("A2.cs0", "A1.yd1", "A2.cd1",),
+    "back": ("A2.cd0",),
+    "b0a": ("out0", "A1.yd0", "A1.xd",),
+    "b0b": ("B0.cs1", "A0.zd",),
+    "b1a": ("out1", "A2.yd1", "B0.cd1",),
+    "b1b": ("B0.cs0",),
+    "b2a": ("A1.zd",),
+    "b2b": ("B1.cs1",),
+    "b3a": ("out2", "B0.cd0", "A2.yd0", "B0.yd1", "A0.zad",),
+    "b3b": ("B1.cs0", "B1.cd1", "A2.xd",),
+    "b4a": ("B1.cd0", "B0.yd0", "A1.zad",),
+    "b4b": ("B2.cs1", "B0.xd",),
+    "b5a": ("B2.cd1", "A2.zd", "A0.yad",),
+    "b5b": ("B2.cs0",),
+    "end1": ("B1.xd", "B0.zd",),
+    "end1b": (),
+    "end2": ("S.cs1", "S.cs0", "S.cd1", "out3", "B2.cd0", "B2.xd", "A2.zad", "S.yd1", "S.cd0", "B1.yd0",
+        "A1.yad", "gin0", "A0.cad",),
+    "drain": ("B0.zad", "B2.yd0", "A1.cad", "gin1", "B1.zd", "gin2", "B2.zd", "A2.yad", "S.yd0", "gin3", "S.xd",
+        "B1.zad", "B0.yad", "A2.cad", "B2.zad", "S.zd", "B0.cad", "B1.yad", "S.zad", "B1.cad", "B2.yad", "S.yad",
+        "B2.cad", "S.cad",),
+}
+WAY = ("yz", "zy", "yz", "yz", "zy")
+XA = (False, False, False)
+XB = (False, True, True)
+FIRST = "oth"
+COUNT = 4
+ORDER = "mix"
 MESH = pl.DeviceIdType.MESH
 NJ = 3
 WA = 256
 WB = 128
-MLP0 = 0
-BACK = 6
-BWD0 = 7
-END = 13
 
 
 def each(n, fn):
@@ -212,7 +260,7 @@
     return (dp // 16 - 1).bit_length()
 
 
-def mlp_chunk(w1, w2, bias, a2, dm, m, da2, hd, piece):
+def mlp_rows(w1, w2, bias, a2, dm, m, da2, hd):
     tot = jnp.zeros((1, CH), F)
     for r in range(T // RT):
         rr = pl.ds(r * RT, RT)
@@ -225,6 +273,10 @@
         m[rr, :] += nn(hb, w2[...])
         da2[rr, :] += nt(du, w1[...])
         tot = tot + jnp.sum(du.astype(F), axis=0, keepdims=True)
+    return tot
+
+
+def mlp_grads(a2, dm, hd, piece):
     for k in range(D // 256):
         g = tn(a2[:, k * 256 : (k + 1) * 256], hd[:, CH : 2 * CH]).astype(B)
         for b in range(CH // WA):
@@ -234,13 +286,21 @@
         g = tn(hd[:, k * 256 : (k + 1) * 256], dm[...]).astype(B)
         for b in range(D // WA):
             piece[base + b * CH + k * 256 : base + b * CH + (k + 1) * 256, :] = g[:, b * WA : (b + 1) * WA]
-    return tot
-
-
-def kernel(dp, lens, inp, cot, g1, s1, wq, bq, wp, bproj, g2, s2, wf, bf, wo, bout,
+
+
+class Row:
+    def __init__(self, ref):
+        self.ref = ref
+
+    def __getitem__(self, _):
+        return self.ref[...].reshape(1, -1)
+
+
+def kernel(dp, lens, inp, cot, wq, bq, wp, wf, wo, g1, s1, bproj, g2, s2, bout, fcb,
            out, gin, gq, gp, gf, go, sm, lf, lo,
-           xf, cf, a1t, wqkv, wproj, bqo, bfo, wb1, wb2, qkv, o, lse, r1, a2, dm, m, da2, hd,
+           xf, cf, a1t, wqkv, wproj, bqo, bfm, bfo, wb1, wb2, qkv, o, lse, r1, a2, dm, m, da2, hd,
            pa, ca, xa, ya, za, ga, pb, xb, yb, zb, ps, cs, xs, ys, zs, gs, ss, rs, ls, ready):
+    g1, s1, bproj, g2, s2, bout = (Row(v) for v in (g1, s1, bproj, g2, s2, bout))
     ti = lax.axis_index("tensor")
     me = lax.axis_index("dp")
     nz = 4
@@ -277,28 +337,29 @@
     def units(group):
         if group == 0:
             return [(wq.at[t], lambda r, t=t: wqkv.at[r, t * D + HW : (t + 1) * D], D) for t in range(3)]
+        if group == 4:
+            return [(wp, lambda r: wproj.at[pl.ds(al(HW + r.start, 16), r.size), :], HW)]
         j = group - 1
         cols = slice(j * CH, (j + 1) * CH)
-        res = [(wf.at[:, cols], lambda r: lf.at[r, cols], D),
-               (wo.at[cols, :], lambda r: lo.at[pl.ds(al(j * CH + r.start, 16), r.size), :], CH)]
-        if group == 1:
-            res.append((wp, lambda r: wproj.at[pl.ds(al(HW + r.start, 16), r.size), :], HW))
-        return res
-
-    wsem = [new(4 * len(units(g))) for g in range(4)]
+        return [(wf.at[:, cols], lambda r: lf.at[r, cols], D),
+                (wo.at[cols, :], lambda r: lo.at[pl.ds(al(j * CH + r.start, 16), r.size), :], CH)]
+
+    wsem = [new(4 * len(units(g))) for g in range(5)]
 
     def wcopies(group, stage):
         res = []
+        first, second = ((z1, Z1), (yy, Y))[:: 1 if WAY[group] == "zy" else -1]
         for i, (own, land, n) in enumerate(units(group)):
             e = n // 8
             if stage < 2:
-                r = pl.ds(al((cc * 4 + yy * 2 + z1) * e, 16), e)
+                r = pl.ds(al((cc * 4 + second[0] * 2 + first[0]) * e, 16), e)
             elif stage == 2:
-                r = pl.ds(al((cc * 2 + yy) * 2 * e, 16), 2 * e)
+                r = pl.ds(al((cc * 2 + second[0]) * 2 * e, 16), 2 * e)
             else:
                 r = pl.ds(al(cc * 4 * e, 16), 4 * e)
             src = own.at[r, :] if stage == 0 else land(r)
-            res.append(rc(src, land(r), wsem[group] + stage * len(units(group)) + i, (X, Z1, Y, C)[stage]))
+            dev = (X, first[1], second[1], C)[stage]
+            res.append(rc(src, land(r), wsem[group] + stage * len(units(group)) + i, dev))
         return res
 
     def wsend(group, stage):
@@ -306,19 +367,25 @@
             c.start()
 
     def wstep(group, stage):
-        for c in wcopies(group, stage):
+        nexts = wcopies(group, stage + 1) if stage < 3 else [None] * len(units(group))
+        for c, d in zip(wcopies(group, stage), nexts):
             c.wait()
-        if stage < 3:
-            wsend(group, stage + 1)
+            if d is not None:
+                d.start()
 
     half = lambda i: pl.ds(al(i * (T // 2), T // 2), T // 2)
-    si = new(8)
+    si = new(12)
     x_copy = rc(inp.at[1 - ti], xf.at[half(ti)], si, X)
     c_copy = rc(cot.at[1 - ti], cf.at[half(ti)], si + 1, X)
     bq_copy = rc(bq, bqo, si + 2, X)
-    bf_copy = rc(bf, bfo, si + 3, X)
-    out_copy = rc(a2.at[half(1 - ti)], out.at[ti], si + 4, X)
-    gin_copy = rc(dm.at[half(1 - ti)], gin.at[ti], si + 5, X)
+    bf_copy = rc(bfm, bfo, si + 3, X)
+    def rows_back(v, res, i):
+        q = T // 2 // COUNT
+        there = lambda b, k: pl.ds(al(b * (T // 2) + k * q, 16), q)
+        return [rc(v.at[there(1 - ti, k)], res.at[ti, k * q : (k + 1) * q], si + i + k, X) for k in range(COUNT)]
+
+    out_copy = rows_back(a2, out, 4)
+    gin_copy = rows_back(dm, gin, 8)
     local = [pltpu.make_async_copy(inp.at[ti], xf.at[half(ti)], ls.at[0]),
              pltpu.make_async_copy(cot.at[ti], cf.at[half(ti)], ls.at[1]),
              pltpu.make_async_copy(wp, wproj.at[0:HW], ls.at[2])]
@@ -328,15 +395,13 @@
     x_copy.start()
     for c in local:
         c.start()
-    bf_copy.start()
-    wsend(1, 0)
-    wsend(2, 0)
-    c_copy.start()
-    wsend(3, 0)
-
-    n = lens[ti, 0]
-
-    def make_set(k_pieces, rows, buf, co, xr, yr, zr, gr, x_first):
+
+    n = lens[0, ti]
+    for j in range(NJ):
+        bfm[j : j + 1, :] = fcb[j * CH : (j + 1) * CH].reshape(1, CH)
+    bfm[NJ:, :] = jnp.zeros((8 - NJ, CH), F)
+
+    def make_set(k_pieces, rows, buf, co, xr, yr, zr, gr, xs_first):
         h, q = rows // 2, rows // 4
         s = q // nz
         base = [new(9 + 4 * nz + len(beyond)) for _ in range(k_pieces)]
@@ -347,16 +412,15 @@
         give = al(cc * h + (1 - yy) * q, 16)
         shard = lambda k: pl.ds(al(keep + k * s, 8), s)
 
-        def swap_c(j):
-            r = pl.ds(al((1 - cc) * h, 16), h)
-            return [rc(buf(w, j, r), co(j, w), base[j] + w, C) for w in (0, 1)]
+        def swap_c(j, w):
+            return rc(buf(w, j, pl.ds(al((1 - cc) * h, 16), h)), co(j, w), base[j] + w, C)
 
         def swap_x(j):
-            src = buf(1, j, pl.ds(mine, h)) if x_first else buf(1, j, pl.ds(keep, q))
-            return [rc(src, xr.at[j], base[j] + 2, X)]
-
-        def swap_y(j):
-            return [rc(buf(w, j, pl.ds(give, q)), yr.at[j, w], base[j] + 3 + w, Y) for w in range(yr.shape[1])]
+            src = buf(1, j, pl.ds(mine, h)) if xs_first[j] else buf(1, j, pl.ds(keep, q))
+            return rc(src, xr(j), base[j] + 2, X)
+
+        def swap_y(j, w):
+            return rc(buf(w, j, pl.ds(give, q)), yr(j, w), base[j] + 3 + w, Y)
 
         def z_out(j):
             each(nz - 1, lambda d: z_one(j, d).start())
@@ -393,57 +457,45 @@
             r = pl.ds(mine, h)
             return rc(buf(0, j, r), buf(0, j, r), base[j] + 6, C)
 
-        def start(cs):
-            for c in cs:
-                c.start()
-
-        def wait(cs):
-            for c in cs:
-                c.wait()
-
         def free(j, i, dev):
             pl.semaphore_signal(ready.at[flag + 3 * j + i], inc=1, device_id=dev, device_id_type=MESH)
 
         def freed(j, i, k):
             pl.semaphore_wait(ready.at[flag + 3 * j + i], k)
 
-        def s0(j):
-            start(swap_c(j))
-
-        def s1_(j):
-            wait(swap_c(j))
-            free(j, 0, C)
-            for w in (1, 0):
-                add_rows(h, buf(w, j, pl.ds(mine, h)), [co(j, w)])
-                if w == 1 and x_first:
-                    start(swap_x(j))
-            if not x_first:
-                start(swap_y(j))
-
-        def s2_(j):
-            if x_first:
-                wait(swap_x(j))
-                add_rows(h, buf(0, j, pl.ds(mine, h)), [xr.at[j]])
-                start(swap_y(j))
+        def cs(j, w):
+            swap_c(j, w).start()
+
+        def cd(j, w):
+            swap_c(j, w).wait()
+            if w == 0:
+                free(j, 0, C)
+            add_rows(h, buf(w, j, pl.ds(mine, h)), [co(j, w)])
+            if not xs_first[j]:
+                swap_y(j, w).start()
+            elif w == 1:
+                swap_x(j).start()
+
+        def yd(j, w):
+            swap_y(j, w).wait()
+            if w == 0:
+                free(j, 1, Y)
+            add_rows(q, buf(w, j, pl.ds(keep, q)), [yr(j, w)])
+            if xs_first[j]:
+                z_out(j)
+            elif w == 1:
+                swap_x(j).start()
+
+        def xd(j):
+            swap_x(j).wait()
+            if xs_first[j]:
+                add_rows(h, buf(0, j, pl.ds(mine, h)), [xr(j)])
+                swap_y(j, 0).start()
             else:
-                wait(swap_y(j))
-                free(j, 1, Y)
-                for w in (1, 0):
-                    add_rows(q, buf(w, j, pl.ds(keep, q)), [yr.at[j, w]])
-                    if w == 1:
-                        start(swap_x(j))
-
-        def s3_(j):
-            if x_first:
-                wait(swap_y(j))
-                free(j, 1, Y)
-                add_rows(q, buf(0, j, pl.ds(keep, q)), [yr.at[j, 0]])
-            else:
-                wait(swap_x(j))
-                add_rows(q, buf(0, j, pl.ds(keep, q)), [xr.at[j]])
-            z_out(j)
-
-        def s4_(j):
+                add_rows(q, buf(0, j, pl.ds(keep, q)), [xr(j)])
+                z_out(j)
+
+        def zd(j):
             z_in(j)
             each(nz - 1, lambda d: free(j, 2, zp(lax.rem(zi + d, nz))))
             add_rows(s, buf(0, j, shard(zi)), [zr.at[j, lax.rem(zi + d, nz)] for d in range(1, nz)])
@@ -455,27 +507,34 @@
             freed(j, 2, nz - 1)
             each(nz - 1, lambda d: za_one(j, d).start())
 
-        def s5_(j):
+        def zad(j):
             za_in(j)
             freed(j, 1, 1)
             all_y(j).start()
 
-        def s6_(j):
+        def yad(j):
             all_y(j).wait()
             freed(j, 0, 1)
             all_c(j).start()
 
-        def s7_(j):
+        def cad(j):
             all_c(j).wait()
 
-        return [s0, s1_, s2_, s3_, s4_, s5_, s6_, s7_]
+        return dict(cs1=lambda j: cs(j, 1), cs0=lambda j: cs(j, 0), cd1=lambda j: cd(j, 1), cd0=lambda j: cd(j, 0),
+                    yd1=lambda j: yd(j, 1), yd0=lambda j: yd(j, 0), xd=xd, zd=zd, zad=zad, yad=yad, cad=cad)
 
     ra = pa.shape[2]
     lanes = slice(0, WB)
-    set_a = make_set(NJ, ra, lambda w, j, r: pa.at[w, j, r], lambda j, w: ca.at[j, w], xa, ya, za, lambda j, b: ga.at[j % 2, b], True)
-    buf_b = lambda w, j, r: pa.at[1, j, r, lanes] if w else pb.at[j, r]
-    set_b = make_set(NJ, ra, buf_b, lambda j, w: ca.at[j, w, :, lanes], xb, yb, zb, lambda j, b: ga.at[(j + 1) % 2, b, :, lanes], False)
-    set_s = make_set(1, ps.shape[2], lambda w, j, r: ps.at[w, j, r], lambda j, w: cs.at[j, w], xs, ys, zs, lambda j, b: gs.at[0, b], False)
+    turns = [v for g in EVENTS.values() for v in g if v.endswith(".zd") and v[0] != "S"]
+    slot = lambda name: turns.index(name) % 2
+    set_a = make_set(NJ, ra, lambda w, j, r: pa.at[w, j, r], lambda j, w: ca.at[j, w],
+                     lambda j: xa.at[j] if XA[j] else xa.at[j, 0 : ra // 4], lambda j, w: ya.at[j, 0] if w == 0 else xa.at[j, ra // 4 :], za, lambda j, b: ga.at[slot(f"A{j}.zd"), b], XA)
+    oth_b = lambda j, r: pa.at[1, j % 2, r, pl.ds(al(j // 2 * WB, WB), WB)]
+    buf_b = lambda w, j, r: oth_b(j, r) if w else pb.at[j, r]
+    set_b = make_set(NJ, ra, buf_b, lambda j, w: ca.at[j, w, :, lanes],
+                     lambda j: xb.at[j] if XB[j] else xb.at[j, 0 : ra // 4], lambda j, w: yb.at[j, 0] if w == 0 else xb.at[j, ra // 4 :], zb, lambda j, b: ga.at[slot(f"B{j}.zd"), b, :, lanes], XB)
+    set_s = make_set(1, ps.shape[2], lambda w, j, r: ps.at[w, j, r], lambda j, w: cs.at[j, w],
+                     lambda j: xs.at[j], lambda j, w: ys.at[j, w], zs, lambda j, b: gs.at[0, b], (False,))
 
     def out_a(j):
         own = pa.at[0, j]
@@ -492,45 +551,37 @@
                 for b in range(D // WB)]
         return [pltpu.make_async_copy(u, v, ls.at[23 + j * 9 + i]) for i, (u, v) in enumerate(res)]
 
-    def a_step(j, s):
+    def step(name):
         def run():
-            set_a[s](j)
-            if s == 7:
-                for c in out_a(j):
+            where, stage = name.split(".")
+            j = int(where[1:] or 0)
+            {"A": set_a, "B": set_b, "S": set_s}[where[0]][stage](j)
+            if stage == "cad":
+                for c in {"A": out_a, "B": out_b, "S": out_s}[where[0]](j):
                     c.start()
         return run
 
-    def b_step(j, s):
-        def run():
-            set_b[s](j)
-            if s == 7:
-                for c in out_b(j):
-                    c.start()
-        return run
-
-    events = {}
-
-    def at(tick, fn):
-        events.setdefault(tick, []).append(fn)
-
-    a_ticks = [[1, 2, 6, 8, 10, 12], [3, 4, 8, 10, 12, 13], [5, 6, 11, 13]]
-    b_ticks = [[8, 9, 11, 13], [10, 11, 13], [12, 13]]
-    pos_a, pos_b = [], []
-    for j in range(NJ):
-        for s, tick in enumerate(a_ticks[j]):
-            at(tick, a_step(j, s))
-        for s, tick in enumerate(b_ticks[j]):
-            at(tick, b_step(j, s))
-        pos_a.append(len(a_ticks[j]))
-        pos_b.append(len(b_ticks[j]))
-
-    def ticks(first, last, t):
-        for g in range(first, last):
-            if g in events:
-                @pl.when(t + first == g)
-                def _(g=g):
-                    for fn in events[g]:
-                        fn()
+    def out_s(j):
+        return [pltpu.make_async_copy(ps.at[0, 0], sm, ls.at[54])]
+
+    def do(names):
+        for name in names:
+            kind, _, rest = name.partition(".")
+            if kind[0] == "W":
+                wstep(int(kind[1:]), int(rest[1:]))
+            elif kind[:3] == "out":
+                out_copy[int(kind[3:])].start()
+            elif kind[:3] == "gin":
+                gin_copy[int(kind[3:])].start()
+            else:
+                step(name)()
+
+    def ticks(where, t):
+        for g, name in enumerate(where):
+            if EVENTS.get(name):
+                @pl.when(t == g)
+                def _(name=name):
+                    do(EVENTS[name])
 
     def put(i, v):
         for w in (0, 1):
@@ -541,9 +592,6 @@
 
     wstep(0, 0)
     wstep(0, 1)
-    local[0].wait()
-    x_copy.wait()
-
     def ln_row(r, _):
         rr = rows_of(r)
         n1, _inv = norm(xf[rr, :].astype(F))
@@ -552,13 +600,24 @@
         a1t[:, rr] = a.T
         return 0
 
-    lax.fori_loop(0, T // RT, ln_row, 0)
+    local[0].wait()
+    own_rows = ti * (T // RT // 2)
+    lax.fori_loop(own_rows, own_rows + T // RT // 2, ln_row, 0)
     wstep(0, 2)
+    x_copy.wait()
+    wsend(4, 0)
+    wsend(1, 0)
+    bf_copy.start()
+    wsend(2, 0)
+    c_copy.start()
+    wsend(3, 0)
+
+    lax.fori_loop(T // RT // 2 - own_rows, T // RT - own_rows, ln_row, 0)
     bq_copy.wait()
     for c in local[3:]:
         c.wait()
     wstep(0, 3)
-    wstep(1, 0)
+    do(EVENTS["ln"])
 
     def qkv_row(r, _):
         rr = rows_of(r)
@@ -572,23 +631,20 @@
                 if t == 0:
                     u = u * 0.125
                 qkv[rr, t * D + k * HW : t * D + (k + 1) * HW] = u.astype(B)
+        ticks(["q0", "q1", "q2", "q3"], r)
         return 0
 
     lax.fori_loop(0, T // RT, qkv_row, 0)
 
     def fwd(hp, _):
         pair_attention(hp, n, qkv, o, lse)
-        for t, fns in ((1, [(1, 1), (2, 0)]), (3, [(2, 1)]), (4, [(1, 2)])):
-            @pl.when(hp == t)
-            def _(fns=fns):
-                for f in fns:
-                    wstep(*f)
+        ticks([f"f{i}" for i in range(6)], hp)
         return 0
 
     lax.fori_loop(0, NP, fwd, 0)
     local[1].wait()
     local[2].wait()
-    wstep(1, 3)
+    do(EVENTS["mid0"])
     c_copy.wait()
     bf_copy.wait()
 
@@ -599,52 +655,50 @@
         return [pltpu.make_async_copy(s1, wb1.at[which], ls.at[50 + which]),
                 pltpu.make_async_copy(s2, wb2.at[which], ls.at[52 + which])]
 
-    for c in fetch(0, 0):
-        c.start()
     phase_mid(n, xf, cf, o, wproj, bproj, g2, s2, r1, a2, dm, put)
     m[...] = jnp.zeros_like(m)
     da2[...] = jnp.zeros_like(da2)
+    do(EVENTS["mid1"])
+    do(EVENTS["mid2"])
+    for c in fetch(1, 0):
+        c.start()
 
     def chunk(t, _):
-        which = lax.rem(t, 2)
+        which = 1 - lax.rem(t, 2)
         j = t // 2
-        for g, fns in ((0, [(2, 2), (3, 0)]), (1, [(2, 3), (3, 1)]), (3, [(3, 2)]), (4, [(3, 3)])):
-            @pl.when(t == g)
-            def _(fns=fns):
-                for f in fns:
-                    wstep(*f)
         for w in (0, 1):
             @pl.when(which == w)
             def _(w=w):
                 for c in fetch(w, j):
                     c.wait()
 
+        bias = jnp.where(which == 0, bfm[pl.ds(j, 1), :], bfo[pl.ds(j, 1), :])
+        tot = mlp_rows(wb1.at[which], wb2.at[which], bias, a2, dm, m, da2, hd)
+        for b in range(CH // 128):
+            ps[which, 0, pl.ds(64 + j * 4 + b, 1), :] = tot[:, b * 128 : (b + 1) * 128]
+        ticks([f"m{i}a" for i in range(6)], t)
+        for w in (0, 1):
             @pl.when((which == 1 - w) & (t < 5))
             def _(w=w):
                 for c in fetch(w, (t + 1) // 2):
                     c.start()
-        bias = jnp.where(which == 0, bf[j], bfo[j])
-        tot = mlp_chunk(wb1.at[which], wb2.at[which], bias, a2, dm, m, da2, hd, pa.at[which, j])
-        for b in range(CH // 128):
-            ps[which, 0, pl.ds(64 + j * 4 + b, 1), :] = tot[:, b * 128 : (b + 1) * 128]
-        ticks(0, 6, t)
+        mlp_grads(a2, dm, hd, pa.at[which, j])
+        ticks([f"m{i}b" for i in range(6)], t)
         return 0
 
     lax.fori_loop(0, 6, chunk, 0)
 
     phase_back(n, cf, r1, m, da2, bout, g2, wproj, dm, hd, a2, put)
-    for fn in events[6]:
-        fn()
-    out_copy.start()
     out_own = pltpu.make_async_copy(a2.at[half(ti)], out.at[ti], ls.at[6])
     gin_own = pltpu.make_async_copy(dm.at[half(ti)], gin.at[ti], ls.at[7])
     out_own.start()
+    do(EVENTS["back"])
 
     def bwd(t, _):
-        which = lax.rem(t, 2)
-        j = t // 2
+        which, j = (1 - t // NJ, lax.rem(t, NJ)) if ORDER == "oth" else (1 - lax.rem(t, 2), t // 2)
         hp = which * NJ + j
         pair_backward(hp, n, qkv, hd, o, lse, m)
+        ticks([f"b{i}a" for i in range(6)], t)
         off = al(hp * 128, 128)
         d = jnp.concatenate([qkv[:, pl.ds(k * D + off, 128)] for k in range(3)], axis=1)
         g = nn(a1t[...], d).astype(B)
@@ -662,46 +716,35 @@
 
         @pl.when(which == 1)
         def _():
-            store(pa.at[1, j, :, lanes])
+            store(oth_b(j, slice(None)))
 
         for k, base in ((0, 48), (2, 56)):
             v = jnp.sum(qkv[:, pl.ds(k * D + off, 128)].astype(F), axis=0, keepdims=True)
             ps[which, 0, pl.ds(base + j, 1), :] = v
-        ticks(7, 13, t)
+        ticks([f"b{i}b" for i in range(6)], t)
         return 0
 
     lax.fori_loop(0, 6, bwd, 0)
-    phase_end(xf, qkv, wqkv, g1, da2, dm, put)
-    set_s[0](0)
-    gin_copy.start()
+    first = (T // RT // 2) * (1 - ti)
+    sums = phase_end(xf, qkv, wqkv, g1, da2, dm, first, None)
+    do(EVENTS["end1"])
+    do(EVENTS["end1b"])
+    a, b = phase_end(xf, qkv, wqkv, g1, da2, dm, T // RT // 2 - first, sums)
+    put(0, a)
+    put(1, b)
     gin_own.start()
-    for fn in events[13]:
-        fn()
-    pos_s = 1
-    for rnd in range(8):
-        for j in range(NJ):
-            if pos_a[j] < 8:
-                a_step(j, pos_a[j])()
-                pos_a[j] += 1
-        for j in range(NJ):
-            if pos_b[j] < 8:
-                b_step(j, pos_b[j])()
-                pos_b[j] += 1
-        if pos_s < 8:
-            set_s[pos_s](0)
-            pos_s += 1
-    sm_own = pltpu.make_async_copy(ps.at[0, 0], sm, ls.at[54])
-    sm_own.start()
+    do(EVENTS["end2"])
+    do(EVENTS["drain"])
     for j in range(NJ):
         for c in out_a(j) + out_b(j):
             c.wait()
-    for c in (sm_own, out_own, gin_own, out_copy, gin_copy):
+    for c in out_s(0) + [out_own, gin_own] + out_copy + gin_copy:
         c.wait()
     assert count[0] <= SEMS(dp)
 
 
 def SEMS(dp):
-    return 48 + 7 * (25 + depth(dp))
+    return 64 + 7 * (25 + depth(dp))
 
 
 def local_call(dp, *args):
@@ -723,13 +766,13 @@
     return pl.pallas_call(
         functools.partial(kernel, dp),
         out_shape=outs,
-        in_specs=[S, A, A, V, V, A, V, A, V, V, V, A, V, A, V],
+        in_specs=[S, A, A, A, V, A, A, A] + [V] * 7,
         out_specs=(A,) * 9,
         scratch_shapes=[
-            vm((T, D), B), vm((T, D), B), vm((D, T), B), vm((D, 3 * D), B), vm((D, D), B), vm((2, HW), F), vm((3, 1, CH), F),
+            vm((T, D), B), vm((T, D), B), vm((D, T), B), vm((D, 3 * D), B), vm((D, D), B), vm((2, HW), F), vm((8, CH), F), vm((8, CH), F),
             vm((2, D, CH), B), vm((2, CH, D), B), vm((T, 3 * D), B), vm((T, D), B), vm((16, T), F), vm((T, D), F),
             vm((T, D), B), vm((T, D), B), vm((T, D), F), vm((T, D), F), vm((T, 2 * CH), B),
-        ] + buffers(NJ, ra, WA, True, B) + [vm((NJ, ra, WB), B)] + buffers(NJ, ra, WB, False, B)[2:5] + buffers(1, rsm, 128, False, F)
+        ] + buffers(NJ, ra, WA, True, B) + [vm((NJ, ra, WB), B)] + buffers(NJ, ra, WB, True, B)[2:5] + buffers(1, rsm, 128, False, F)
         + [sem((SEMS(dp),)), sem((SEMS(dp),)), sem((56,)), pltpu.SemaphoreType.REGULAR((21,))],
         compiler_params=pltpu.CompilerParams(vmem_limit_bytes=VLIMIT, collective_id=0, has_side_effects=True),
     )(*args)
@@ -740,16 +783,78 @@
 
 def body(dp, inputs, cotangent, lengths, gain_one, shift_one, qkv_weight, qv_bias, proj_weight, proj_bias, gain_two,
          shift_two, fc_weight, fc_bias, out_weight, out_bias):
-    row = lambda v: v.reshape(1, D)
-    out, gin, gq, gp, gf, go, sm, _lf, _lo = local_call(
-        dp, lengths, inputs.reshape(2, T // 2, D), cotangent.reshape(2, T // 2, D), row(gain_one), row(shift_one),
-        jnp.transpose(qkv_weight, (1, 0, 2)), qv_bias, proj_weight, row(proj_bias), row(gain_two), row(shift_two),
-        fc_weight, fc_bias.reshape(3, 1, CH), out_weight, row(out_bias))
-    vec = lambda i: sm[i * 8 : i * 8 + 6].reshape(D)
-    gqv = jnp.stack([sm[48:51].reshape(HW), sm[56:59].reshape(HW)])
-    rows = lambda v: v.astype(F)[:, None]
-    return (rows(out), rows(gin), vec(0), vec(1), jnp.transpose(gq.astype(F), (1, 0, 2)), gqv, gp.astype(F), vec(2), vec(3),
-            vec(4), gf.astype(F), sm[64:76].reshape(FH), go.astype(F), vec(5))
+    res = local_call(
+        dp, lengths.reshape(1, 2), inputs.reshape(2, T // 2, D), cotangent.reshape(2, T // 2, D),
+        jnp.transpose(qkv_weight, (1, 0, 2)), qv_bias, proj_weight, fc_weight, out_weight, gain_one, shift_one,
+        proj_bias, gain_two, shift_two, out_bias, fc_bias)
+    out, gin, gq, gp, gf, go, gqv, gfb, *vec = widen(*res[:7])
+    rows = lambda v: v[:, None]
+    return (rows(out), rows(gin), vec[0], vec[1], jnp.transpose(gq, (1, 0, 2)), gqv, gp, vec[2], vec[3], vec[4], gf, gfb,
+            go, vec[5])
+
+
+def widen_kernel(*refs):
+    srcs, sm, dsts, (gqv, gfb, *vec), (ins, outs, si, so) = refs[:6], refs[6], refs[7:13], refs[13:21], refs[21:]
+    tiles = []
+    for s, d in zip(srcs, dsts):
+        for a in range(s.shape[0] if len(s.shape) == 3 else 1):
+            u, v = (s.at[a], d.at[a]) if len(s.shape) == 3 else (s, d)
+            step = min(512, u.shape[0])
+            for b in range(0, u.shape[0], step):
+                tiles.append((u.at[b : b + step], v.at[b : b + step], u.shape[1], min(step, u.shape[0] - b)))
+    place, row, col = [], 0, 0
+    for _u, _v, wide, n in tiles:
+        if col + wide > FH:
+            row, col = row + 1, 0
+        place.append((row, pl.ds(0, n), pl.ds(col, wide)))
+        col += wide
+    def load(i):
+        r, a, b = place[i]
+        return pltpu.make_async_copy(tiles[i][0], ins.at[r, a, b], si.at[i])
+    def save(i):
+        r, a, b = place[i]
+        return pltpu.make_async_copy(outs.at[r, a, b], tiles[i][1], so.at[i])
+    for i in range(len(tiles)):
+        load(i).start()
+    for i in range(6):
+        for b in range(D // 128):
+            vec[i][b * 128 : (b + 1) * 128] = sm[i * 8 + b, :]
+    for b in range(FH // 128):
+        gfb[b * 128 : (b + 1) * 128] = sm[64 + b, :]
+    for b in range(HW // 128):
+        gqv[0:1, b * 128 : (b + 1) * 128] = sm[48 + b : 49 + b, :]
+        gqv[1:2, b * 128 : (b + 1) * 128] = sm[56 + b : 57 + b, :]
+    for i in range(len(tiles)):
+        load(i).wait()
+        r, _a, b = place[i]
+        n = tiles[i][3]
+
+        def step(k, _):
+            rr = pl.ds(pl.multiple_of(k * 64, 64), 64)
+            outs[r, rr, b] = ins[r, rr, b].astype(F)
+            return 0
+
+        lax.fori_loop(0, n // 64, step, 0)
+        save(i).start()
+    for i in range(len(tiles)):
+        save(i).wait()
+
+
+def widen(*args):
+    V = pl.BlockSpec(memory_space=pltpu.VMEM)
+    A = pl.BlockSpec(memory_space=pl.ANY)
+    sd = jax.ShapeDtypeStruct
+    wide = [sd(v.shape, F) for v in args[:6]]
+    small = [sd((2, HW), F), sd((FH,), F)] + [sd((D,), F)] * 6
+    sem = pltpu.SemaphoreType.DMA
+    return pl.pallas_call(
+        widen_kernel,
+        out_shape=tuple(wide + small),
+        in_specs=[A] * 6 + [V],
+        out_specs=tuple([A] * 6 + [V] * 8),
+        scratch_shapes=[pltpu.VMEM((9, 512, FH), B), pltpu.VMEM((9, 512, FH), F), sem((24,)), sem((24,))],
+        compiler_params=pltpu.CompilerParams(vmem_limit_bytes=56 * 2**20),
+    )(*args)
 
 
 def solution(mesh):

time: 259 us -> 213 us (0.82)
  Pallas kernels: 230 us -> 212 us
  other arithmetic: 14.3 us -> 0 us
  local copies, waits for them, and re-layouts: 13.5 us -> 0 us
    pallas_call x1, Pallas kernels: 230 us -> 201 us  [local_call(): pl.pallas_call(functools.partial(kernel, dp), out_shape=outs, in_specs=[S...]
    pallas_call x0 -> x1, Pallas kernels: none -> 11.6 us  [widen(): pl.pallas_call(widen_kernel, out_shape=tuple(wide + small), in_specs=[A]...]
    reshape x9 -> x0, local copies, waits for them, and re-layouts: 11.5 us -> none  [the longest x6 7.6 us: body(): row = lambda v: v.reshape(1, D)]
    convert_element_type x3 -> x0, other arithmetic: 6.47 us -> none  [the longest x1 2.83 us: body(): gf.astype(F)]
    unnamed x1 -> x0, other arithmetic: 5.27 us -> none
where the time goes in v3:
time: 213 us
  Pallas kernels  212 us (100%)
    pallas_call x1, Pallas kernels, local_call(): pl.pallas_call(functools.partial(kernel, dp), out_shape=outs, in_specs=[S...  201 us
    pallas_call x1, Pallas kernels, widen(): pl.pallas_call(widen_kernel, out_shape=tuple(wide + small), in_specs=[A]...  11.6 us

profile of v3, /device:TPU:0, one launch (start us, length us, event | category | flops | bytes accessed | tf_op | source)
XLA Modules:
  0.0 213.2 jit_solution(3253492559703229071)
XLA Ops:
  0.7 200.8 %shard_map.254 = (bf16[2,512,768]{2,1,0:T(8,128)(2,1)}, bf16[2,512,768]{2,1,0:T(8,128)(2,1)}, bf16[3,768,384]{2,1,0:T(8,128)(2,1)}, bf16[384,768]{1,0:T(8,128)(2...) custom-call(s32[1,2]{1,0:T(1,128)} %bitcast.14, ...), custom_call_target="tpu_custom_call" | custom-call | tf_op jit(solution)/shard_map/pallas_call | solution.py:766
  201.5 11.6 %shard_map.255 = (f32[2,512,768]{2,1,0:T(8,128)}, f32[2,512,768]{2,1,0:T(8,128)}, f32[3,768,384]{2,1,0:T(8,128)}, f32[384,768]{1,0:T(8,128)}, f32[768,1536]{1,0:...) custom-call(bf16[2,512,768]{2,1,0:T(8,128)(2,1)} %get-tuple-element., ...), custom_call_target="tpu_custom_call" | custom-call | tf_op jit(solution)/shard_map/pallas_call | solution.py:850

commit v4 on v3

--- a/solution.py
+++ b/solution.py
@@ -122,19 +122,27 @@
     qkv[:, pl.ds(2 * D + off, 128)] = acc[:, 128:256].astype(B)
 
 
-def phase_mid(n, x, c, o, wproj, bproj, g2, s2, r1, a2, dm, put):
-    def row(r, ob):
+def phase_mid(x, o, wproj, bproj, g2, s2, r1, a2):
+    def row(r, _):
         rr = rows_of(r)
         v = x[rr, :].astype(F) + SB * (nn(o[rr, :], wproj[...]) + bproj[...])
         r1[rr, :] = v
         n2, _inv = norm(v)
         a2[rr, :] = (n2 * g2[...] + s2[...]).astype(B)
+        return 0
+
+    lax.fori_loop(0, T // RT, row, 0)
+
+
+def phase_cot(n, c, dm):
+    def row(r, ob):
+        rr = rows_of(r)
         ids = lax.broadcasted_iota(jnp.int32, (RT, 1), 0) + r * RT
         cs = SB * (c[rr, :].astype(F) * (ids < n).astype(F))
         dm[rr, :] = cs.astype(B)
         return ob + jnp.sum(cs, axis=0, keepdims=True)
 
-    put(5, lax.fori_loop(0, T // RT, row, jnp.zeros((1, D), F)))
+    return lax.fori_loop(0, T // RT, row, jnp.zeros((1, D), F))
 
 
 def phase_back(n, c, r1, m, da2, bout, g2, wproj, dattn, do, out, put):
@@ -176,58 +184,60 @@
 
 EVENTS = {
     "ln": (),
-    "q0": ("W4.w0",),
+    "q0": (),
     "q1": (),
     "q2": (),
-    "q3": (),
-    "f0": ("W1.w0", "W4.w1",),
-    "f1": ("W2.w0",),
-    "f2": ("W1.w1", "W4.w2",),
-    "f3": ("W2.w1", "W4.w3",),
-    "f4": (),
-    "f5": ("W1.w2",),
+    "q3": ("W1.w0",),
+    "f0": ("W4.w0",),
+    "f1": ("W2.w0", "W1.w1",),
+    "f2": ("W3.w0", "W4.w1",),
+    "f3": ("W2.w1",),
+    "f4": ("W4.w2",),
+    "f5": ("W1.w2", "W4.w3",),
     "mid0": (),
-    "mid1": ("W3.w0", "W2.w2",),
+    "mid1": ("W2.w2",),
     "mid2": ("W1.w3",),
-    "m0a": (),
-    "m0b": ("A0.cs1", "W3.w1", "W2.w3",),
-    "m1a": ("A0.cd1",),
-    "m1b": ("A0.cs0",),
-    "m2a": ("W3.w2", "A0.cd0",),
-    "m2b": ("A1.cs1",),
+    "m0a": ("W3.w1", "W2.w3",),
+    "m0b": ("A0.cs1",),
+    "m1a": (),
+    "m1b": ("A0.cs0", "A0.cd1",),
+    "m2a": ("W3.w2",),
+    "m2b": ("A1.cs1", "A0.cd0",),
     "m3a": ("W3.w3", "A0.yd1",),
     "m3b": ("A1.cs0", "A1.cd1",),
-    "m4a": ("A0.yd0",),
-    "m4b": ("A2.cs1", "A1.cd0",),
-    "m5a": ("A0.xd",),
-    "m5b": ("A2.cs0", "A1.yd1", "A2.cd1",),
-    "back": ("A2.cd0",),
-    "b0a": ("out0", "A1.yd0", "A1.xd",),
-    "b0b": ("B0.cs1", "A0.zd",),
-    "b1a": ("out1", "A2.yd1", "B0.cd1",),
-    "b1b": ("B0.cs0",),
-    "b2a": ("A1.zd",),
-    "b2b": ("B1.cs1",),
-    "b3a": ("out2", "B0.cd0", "A2.yd0", "B0.yd1", "A0.zad",),
-    "b3b": ("B1.cs0", "B1.cd1", "A2.xd",),
-    "b4a": ("B1.cd0", "B0.yd0", "A1.zad",),
-    "b4b": ("B2.cs1", "B0.xd",),
-    "b5a": ("B2.cd1", "A2.zd", "A0.yad",),
-    "b5b": ("B2.cs0",),
-    "end1": ("B1.xd", "B0.zd",),
+    "m4a": ("A1.cd0", "A0.yd0",),
+    "m4b": ("A2.cs1", "A0.xd",),
+    "m5a": (),
+    "m5b": ("A2.cs0", "A2.cd1", "A1.yd1",),
+    "back": ("A2.cd0", "A0.zd",),
+    "proj": ("P.cs1", "P.cs0",),
+    "b0a": ("out0", "A1.yd0", "A1.xd", "P.cd1", "P.cd0",),
+    "b0b": ("B0.cs1",),
+    "b1a": ("A2.yd1", "A0.zad",),
+    "b1b": ("B1.cs1",),
+    "b2a": ("A2.yd0", "A1.zd", "B0.cd1", "P.xd", "B1.cd1",),
+    "b2b": ("B2.cs1",),
+    "b3a": ("B2.cd1",),
+    "b3b": ("B0.cs0", "A2.xd", "A0.yad",),
+    "b4a": ("B0.cd0", "P.yd0", "A1.zad",),
+    "b4b": ("B1.cs0", "A0.cad",),
+    "b5a": ("A2.zd", "B1.cd0", "B0.xd", "B1.xd",),
+    "b5b": ("B2.cs0", "A1.yad", "out1", "B2.cd0", "P.zd",),
+    "end1": ("B2.xd", "out2", "B0.yd0",),
     "end1b": (),
-    "end2": ("S.cs1", "S.cs0", "S.cd1", "out3", "B2.cd0", "B2.xd", "A2.zad", "S.yd1", "S.cd0", "B1.yd0",
-        "A1.yad", "gin0", "A0.cad",),
-    "drain": ("B0.zad", "B2.yd0", "A1.cad", "gin1", "B1.zd", "gin2", "B2.zd", "A2.yad", "S.yd0", "gin3", "S.xd",
-        "B1.zad", "B0.yad", "A2.cad", "B2.zad", "S.zd", "B0.cad", "B1.yad", "S.zad", "B1.cad", "B2.yad", "S.yad",
-        "B2.cad", "S.cad",),
+    "end2": ("S.cs1", "S.cs0", "A1.cad", "B1.yd0",),
+    "drain": ("A2.zad", "out3", "S.cd1", "P.zad", "B2.yd0", "S.cd0", "B0.zd", "gin0", "B1.zd", "gin1", "A2.yad",
+        "S.yd1", "B2.zd", "P.yad", "gin2", "B0.zad", "S.yd0", "A2.cad", "S.xd", "B1.zad", "P.cad", "gin3",
+        "B0.yad", "B2.zad", "S.zd", "B1.yad", "B0.cad", "S.zad", "B2.yad", "B1.cad", "S.yad", "B2.cad", "S.cad",),
 }
-WAY = ("yz", "zy", "yz", "yz", "zy")
+WAY = ("zy", "zy", "yz", "yz", "yz")
 XA = (False, False, False)
-XB = (False, True, True)
+XB = (True, True, True)
+XP = (True,)
 FIRST = "oth"
+AFTER = (1, 4, 2, 3, 0)
 COUNT = 4
-ORDER = "mix"
+ORDER = "oth"
 MESH = pl.DeviceIdType.MESH
 NJ = 3
 WA = 256
@@ -299,7 +309,7 @@
 def kernel(dp, lens, inp, cot, wq, bq, wp, wf, wo, g1, s1, bproj, g2, s2, bout, fcb,
            out, gin, gq, gp, gf, go, sm, lf, lo,
            xf, cf, a1t, wqkv, wproj, bqo, bfm, bfo, wb1, wb2, qkv, o, lse, r1, a2, dm, m, da2, hd,
-           pa, ca, xa, ya, za, ga, pb, xb, yb, zb, ps, cs, xs, ys, zs, gs, ss, rs, ls, ready):
+           pa, ca, xa, ya, za, ga, pb, xb, yb, zb, pp, op, cp, xp, yp, zp_, ps, cs, xs, ys, zs, gs, ss, rs, ls, ready):
     g1, s1, bproj, g2, s2, bout = (Row(v) for v in (g1, s1, bproj, g2, s2, bout))
     ti = lax.axis_index("tensor")
     me = lax.axis_index("dp")
@@ -427,13 +437,13 @@
 
         def z_one(j, d):
             k = lax.rem(zi + d, nz)
-            return rc(buf(0, j, shard(k)), zr.at[j, zi], base[j] + 9 + k, zp(k), base[j] + 9 + nz + zi)
+            return rc(buf(0, j, shard(k)), zr(j, zi), base[j] + 9 + k, zp(k), base[j] + 9 + nz + zi)
 
         def z_in(j):
             def one(d):
                 z_one(j, d).wait_send()
                 k = lax.rem(zi + d, nz)
-                rc(zr.at[j, k], zr.at[j, k], base[j] + 9 + k, zp(k), base[j] + 9 + nz + k).wait_recv()
+                rc(zr(j, k), zr(j, k), base[j] + 9 + k, zp(k), base[j] + 9 + nz + k).wait_recv()
 
             each(nz - 1, one)
 
@@ -498,7 +508,7 @@
         def zd(j):
             z_in(j)
             each(nz - 1, lambda d: free(j, 2, zp(lax.rem(zi + d, nz))))
-            add_rows(s, buf(0, j, shard(zi)), [zr.at[j, lax.rem(zi + d, nz)] for d in range(1, nz)])
+            add_rows(s, buf(0, j, shard(zi)), [zr(j, lax.rem(zi + d, nz)) for d in range(1, nz)])
             for b, dev in enumerate(beyond):
                 copy = rc(buf(0, j, shard(zi)), gr(j, b), base[j] + 9 + 4 * nz + b, dev)
                 copy.start()
@@ -528,13 +538,23 @@
     turns = [v for g in EVENTS.values() for v in g if v.endswith(".zd") and v[0] != "S"]
     slot = lambda name: turns.index(name) % 2
     set_a = make_set(NJ, ra, lambda w, j, r: pa.at[w, j, r], lambda j, w: ca.at[j, w],
-                     lambda j: xa.at[j] if XA[j] else xa.at[j, 0 : ra // 4], lambda j, w: ya.at[j, 0] if w == 0 else xa.at[j, ra // 4 :], za, lambda j, b: ga.at[slot(f"A{j}.zd"), b], XA)
+                     lambda j: xa.at[j] if XA[j] else xa.at[j, 0 : ra // 4], lambda j, w: ya.at[j, 0] if w == 0 else xa.at[j, ra // 4 :], lambda j, k: za.at[j, k], lambda j, b: ga.at[slot(f"A{j}.zd"), b], XA)
+    rb, b4 = pb.shape[1], pb.shape[1] // 4
     oth_b = lambda j, r: pa.at[1, j % 2, r, pl.ds(al(j // 2 * WB, WB), WB)]
-    buf_b = lambda w, j, r: oth_b(j, r) if w else pb.at[j, r]
-    set_b = make_set(NJ, ra, buf_b, lambda j, w: ca.at[j, w, :, lanes],
-                     lambda j: xb.at[j] if XB[j] else xb.at[j, 0 : ra // 4], lambda j, w: yb.at[j, 0] if w == 0 else xb.at[j, ra // 4 :], zb, lambda j, b: ga.at[slot(f"B{j}.zd"), b, :, lanes], XB)
+
+    def buf_b(w, j, r):
+        return oth_b(j, r) if w else pb.at[j, r]
+
+    set_b = make_set(NJ, rb, buf_b, lambda j, w: ca.at[j, w, 0 : 2 * b4, lanes],
+                     lambda j: xb.at[j] if XB[j] else xb.at[j, 0:b4], lambda j, w: yb.at[j, 0] if w == 0 else xb.at[j, b4:],
+                     lambda j, k: zb.at[j, k],
+                     lambda j, b: ga.at[slot(f"B{j}.zd"), b, 0 : zb.shape[2], lanes], XB)
+    set_p = make_set(1, rb, lambda w, j, r: op.at[r] if w else pp.at[r], lambda j, w: cp.at[w],
+                     lambda j: xp.at[0] if XP[0] else xp.at[0, 0:b4], lambda j, w: yp.at[0, 0] if w == 0 else xp.at[0, b4:],
+                     lambda j, k: zp_.at[0, k],
+                     lambda j, b: ga.at[slot("P.zd"), b, 0 : zb.shape[2], lanes], XP)
     set_s = make_set(1, ps.shape[2], lambda w, j, r: ps.at[w, j, r], lambda j, w: cs.at[j, w],
-                     lambda j: xs.at[j], lambda j, w: ys.at[j, w], zs, lambda j, b: gs.at[0, b], (False,))
+                     lambda j: xs.at[j], lambda j, w: ys.at[j, w], lambda j, k: zs.at[j, k], lambda j, b: gs.at[0, b], (False,))
 
     def out_a(j):
         own = pa.at[0, j]
@@ -547,17 +567,18 @@
     def out_b(j):
         own = pb.at[j]
         res = [(own.at[t * D : (t + 1) * D], gq.at[t, :, j * WB : (j + 1) * WB]) for t in range(3)]
-        res += [(own.at[3 * D + b * WB : 3 * D + (b + 1) * WB], gp.at[j * WB : (j + 1) * WB, b * WB : (b + 1) * WB])
-                for b in range(D // WB)]
         return [pltpu.make_async_copy(u, v, ls.at[23 + j * 9 + i]) for i, (u, v) in enumerate(res)]
+
+    def out_p(j):
+        return [pltpu.make_async_copy(pp.at[b * HW : (b + 1) * HW], gp.at[:, b * WB : (b + 1) * WB], ls.at[56 + b]) for b in range(D // WB)]
 
     def step(name):
         def run():
             where, stage = name.split(".")
             j = int(where[1:] or 0)
-            {"A": set_a, "B": set_b, "S": set_s}[where[0]][stage](j)
+            {"A": set_a, "B": set_b, "S": set_s, "P": set_p}[where[0]][stage](j)
             if stage == "cad":
-                for c in {"A": out_a, "B": out_b, "S": out_s}[where[0]](j):
+                for c in {"A": out_a, "B": out_b, "S": out_s, "P": out_p}[where[0]](j):
                     c.start()
         return run
 
@@ -605,12 +626,12 @@
     lax.fori_loop(own_rows, own_rows + T // RT // 2, ln_row, 0)
     wstep(0, 2)
     x_copy.wait()
-    wsend(4, 0)
-    wsend(1, 0)
     bf_copy.start()
-    wsend(2, 0)
-    c_copy.start()
-    wsend(3, 0)
+    for g in AFTER:
+        if g:
+            wsend(g, 0)
+        else:
+            c_copy.start()
 
     lax.fori_loop(T // RT // 2 - own_rows, T // RT - own_rows, ln_row, 0)
     bq_copy.wait()
@@ -645,7 +666,6 @@
     local[1].wait()
     local[2].wait()
     do(EVENTS["mid0"])
-    c_copy.wait()
     bf_copy.wait()
 
     def fetch(which, j):
@@ -655,10 +675,12 @@
         return [pltpu.make_async_copy(s1, wb1.at[which], ls.at[50 + which]),
                 pltpu.make_async_copy(s2, wb2.at[which], ls.at[52 + which])]
 
-    phase_mid(n, xf, cf, o, wproj, bproj, g2, s2, r1, a2, dm, put)
+    phase_mid(xf, o, wproj, bproj, g2, s2, r1, a2)
     m[...] = jnp.zeros_like(m)
     da2[...] = jnp.zeros_like(da2)
     do(EVENTS["mid1"])
+    c_copy.wait()
+    put(5, phase_cot(n, cf, dm))
     do(EVENTS["mid2"])
     for c in fetch(1, 0):
         c.start()
@@ -693,6 +715,11 @@
     gin_own = pltpu.make_async_copy(dm.at[half(ti)], gin.at[ti], ls.at[7])
     out_own.start()
     do(EVENTS["back"])
+    for w, piece in ((1, op), (0, pp)):
+        g = tn(o[:, w * HW : (w + 1) * HW], dm[...]).astype(B)
+        for b in range(D // WB):
+            piece[b * HW : (b + 1) * HW, :] = g[:, b * WB : (b + 1) * WB]
+    do(EVENTS["proj"])
 
     def bwd(t, _):
         which, j = (1 - t // NJ, lax.rem(t, NJ)) if ORDER == "oth" else (1 - lax.rem(t, 2), t // 2)
@@ -702,13 +729,10 @@
         off = al(hp * 128, 128)
         d = jnp.concatenate([qkv[:, pl.ds(k * D + off, 128)] for k in range(3)], axis=1)
         g = nn(a1t[...], d).astype(B)
-        e = tn(o[:, pl.ds(off, 128)], dm[...]).astype(B)
 
         def store(piece):
             for k in range(3):
                 piece[k * D : (k + 1) * D, :] = g[:, k * 128 : (k + 1) * 128]
-            for b in range(D // WB):
-                piece[3 * D + b * WB : 3 * D + (b + 1) * WB, :] = e[:, b * WB : (b + 1) * WB]
 
         @pl.when(which == 0)
         def _():
@@ -716,7 +740,7 @@
 
         @pl.when(which == 1)
         def _():
-            store(oth_b(j, slice(None)))
+            store(oth_b(j, slice(0, rb)))
 
         for k, base in ((0, 48), (2, 56)):
             v = jnp.sum(qkv[:, pl.ds(k * D + off, 128)].astype(F), axis=0, keepdims=True)
@@ -738,13 +762,13 @@
     for j in range(NJ):
         for c in out_a(j) + out_b(j):
             c.wait()
-    for c in out_s(0) + [out_own, gin_own] + out_copy + gin_copy:
+    for c in out_s(0) + out_p(0) + [out_own, gin_own] + out_copy + gin_copy:
         c.wait()
     assert count[0] <= SEMS(dp)
 
 
 def SEMS(dp):
-    return 64 + 7 * (25 + depth(dp))
+    return 64 + 8 * (25 + depth(dp))
 
 
 def local_call(dp, *args):
@@ -752,7 +776,7 @@
     S = pl.BlockSpec(memory_space=pltpu.SMEM)
     A = pl.BlockSpec(memory_space=pl.ANY)
     sd = jax.ShapeDtypeStruct
-    ra, rsm, nz = 4 * D, 256, 4
+    ra, rb, rsm, nz = 4 * D, 3 * D, 256, 4
     nb = max(depth(dp), 1)
     outs = (sd((2, T // 2, D), B), sd((2, T // 2, D), B), sd((3, D, HW), B), sd((HW, D), B), sd((D, FH), B),
             sd((FH, D), B), sd((rsm, 128), F), sd((D, FH), B), sd((FH, D), B))
@@ -772,8 +796,9 @@
             vm((T, D), B), vm((T, D), B), vm((D, T), B), vm((D, 3 * D), B), vm((D, D), B), vm((2, HW), F), vm((8, CH), F), vm((8, CH), F),
             vm((2, D, CH), B), vm((2, CH, D), B), vm((T, 3 * D), B), vm((T, D), B), vm((16, T), F), vm((T, D), F),
             vm((T, D), B), vm((T, D), B), vm((T, D), F), vm((T, D), F), vm((T, 2 * CH), B),
-        ] + buffers(NJ, ra, WA, True, B) + [vm((NJ, ra, WB), B)] + buffers(NJ, ra, WB, True, B)[2:5] + buffers(1, rsm, 128, False, F)
-        + [sem((SEMS(dp),)), sem((SEMS(dp),)), sem((56,)), pltpu.SemaphoreType.REGULAR((21,))],
+        ] + buffers(NJ, ra, WA, True, B) + [vm((NJ, rb, WB), B)] + buffers(NJ, rb, WB, True, B)[2:5]
+        + [vm((rb, WB), B), vm((rb, WB), B), vm((2, rb // 2, WB), B)] + buffers(1, rb, WB, True, B)[2:5] + buffers(1, rsm, 128, False, F)
+        + [sem((SEMS(dp),)), sem((SEMS(dp),)), sem((64,)), pltpu.SemaphoreType.REGULAR((24,))],
         compiler_params=pltpu.CompilerParams(vmem_limit_bytes=VLIMIT, collective_id=0, has_side_effects=True),
     )(*args)
 

time: 213 us -> 210 us (0.986)
  Pallas kernels: 212 us -> 209 us
    pallas_call x1, Pallas kernels: 201 us -> 197 us  [local_call(): pl.pallas_call(functools.partial(kernel, dp), out_shape=outs, in_specs=[S...]
where the time goes in v4:
time: 210 us
  Pallas kernels  209 us (100%)
    pallas_call x1, Pallas kernels, local_call(): pl.pallas_call(functools.partial(kernel, dp), out_shape=outs, in_specs=[S...  197 us
    pallas_call x1, Pallas kernels, widen(): pl.pallas_call(widen_kernel, out_shape=tuple(wide + small), in_specs=[A]...  11.6 us

profile of v4, /device:TPU:0, one launch (start us, length us, event | category | flops | bytes accessed | tf_op | source)
XLA Modules:
  0.0 209.7 jit_solution(10176090740724847848)
XLA Ops:
  0.7 197.3 %shard_map.254 = (bf16[2,512,768]{2,1,0:T(8,128)(2,1)}, bf16[2,512,768]{2,1,0:T(8,128)(2,1)}, bf16[3,768,384]{2,1,0:T(8,128)(2,1)}, bf16[384,768]{1,0:T(8,128)(2...) custom-call(s32[1,2]{1,0:T(1,128)} %bitcast.14, ...), custom_call_target="tpu_custom_call" | custom-call | tf_op jit(solution)/shard_map/pallas_call | solution.py:790
  198.0 11.6 %shard_map.255 = (f32[2,512,768]{2,1,0:T(8,128)}, f32[2,512,768]{2,1,0:T(8,128)}, f32[3,768,384]{2,1,0:T(8,128)}, f32[384,768]{1,0:T(8,128)}, f32[768,1536]{1,0:...) custom-call(bf16[2,512,768]{2,1,0:T(8,128)(2,1)} %get-tuple-element., ...), custom_call_target="tpu_custom_call" | custom-call | tf_op jit(solution)/shard_map/pallas_call | solution.py:875

commit v5 on v4

--- a/solution.py
+++ b/solution.py
@@ -637,14 +637,10 @@
     bq_copy.wait()
     for c in local[3:]:
         c.wait()
-    wstep(0, 3)
-    do(EVENTS["ln"])
-
-    def qkv_row(r, _):
-        rr = rows_of(r)
-        a = a2[rr, :]
-        for t in range(3):
-            v = nn(a, wqkv[:, t * D : (t + 1) * D])
+    def qkv_rows(t):
+        def row(r, _):
+            rr = rows_of(r)
+            v = nn(a2[rr, :], wqkv[:, t * D : (t + 1) * D])
             for k, b in enumerate((bq, bqo)):
                 u = v[:, k * HW : (k + 1) * HW]
                 if t != 1:
@@ -652,10 +648,15 @@
                 if t == 0:
                     u = u * 0.125
                 qkv[rr, t * D + k * HW : t * D + (k + 1) * HW] = u.astype(B)
-        ticks(["q0", "q1", "q2", "q3"], r)
-        return 0
-
-    lax.fori_loop(0, T // RT, qkv_row, 0)
+            return 0
+
+        wcopies(0, 3)[t].wait()
+        lax.fori_loop(0, T // RT, row, 0)
+
+    for t, names in enumerate((("ln", "q0"), ("q1",), ("q2", "q3"))):
+        qkv_rows(t)
+        for name in names:
+            do(EVENTS[name])
 
     def fwd(hp, _):
         pair_attention(hp, n, qkv, o, lse)
@@ -824,7 +825,7 @@
     for s, d in zip(srcs, dsts):
         for a in range(s.shape[0] if len(s.shape) == 3 else 1):
             u, v = (s.at[a], d.at[a]) if len(s.shape) == 3 else (s, d)
-            step = min(512, u.shape[0])
+            step = min(256, u.shape[0])
             for b in range(0, u.shape[0], step):
                 tiles.append((u.at[b : b + step], v.at[b : b + step], u.shape[1], min(step, u.shape[0] - b)))
     place, row, col = [], 0, 0
@@ -877,7 +878,7 @@
         out_shape=tuple(wide + small),
         in_specs=[A] * 6 + [V],
         out_specs=tuple([A] * 6 + [V] * 8),
-        scratch_shapes=[pltpu.VMEM((9, 512, FH), B), pltpu.VMEM((9, 512, FH), F), sem((24,)), sem((24,))],
+        scratch_shapes=[pltpu.VMEM((18, 256, FH), B), pltpu.VMEM((18, 256, FH), F), sem((40,)), sem((40,))],
         compiler_params=pltpu.CompilerParams(vmem_limit_bytes=56 * 2**20),
     )(*args)
 

time: 210 us -> 210 us (level)
  no operation moved by 1% of the time
where the time goes in v5:
time: 210 us
  Pallas kernels  209 us (100%)
    pallas_call x1, Pallas kernels, local_call(): pl.pallas_call(functools.partial(kernel, dp), out_shape=outs, in_specs=[S...  197 us
    pallas_call x1, Pallas kernels, widen(): pl.pallas_call(widen_kernel, out_shape=tuple(wide + small), in_specs=[A]...  11.9 us

profile of v5, /device:TPU:0, one launch (start us, length us, event | category | flops | bytes accessed | tf_op | source)
XLA Modules:
  0.0 210.1 jit_solution(17347046719514446757)
XLA Ops:
  0.7 197.3 %shard_map.254 = (bf16[2,512,768]{2,1,0:T(8,128)(2,1)}, bf16[2,512,768]{2,1,0:T(8,128)(2,1)}, bf16[3,768,384]{2,1,0:T(8,128)(2,1)}, bf16[384,768]{1,0:T(8,128)(2...) custom-call(s32[1,2]{1,0:T(1,128)} %bitcast.14, ...), custom_call_target="tpu_custom_call" | custom-call | tf_op jit(solution)/shard_map/pallas_call | solution.py:791
  198.0 11.9 %shard_map.255 = (f32[2,512,768]{2,1,0:T(8,128)}, f32[2,512,768]{2,1,0:T(8,128)}, f32[3,768,384]{2,1,0:T(8,128)}, f32[384,768]{1,0:T(8,128)}, f32[768,1536]{1,0:...) custom-call(bf16[2,512,768]{2,1,0:T(8,128)(2,1)} %get-tuple-element., ...), custom_call_target="tpu_custom_call" | custom-call | tf_op jit(solution)/shard_map/pallas_call | solution.py:876
